TPU v7x, 512 devices: a whole 4x4x16 slice. The times are simulated.
512 devices in a mesh: blk: 8 (over z_lo), tok: 64 (over z_hi, x, y, core).
Axes of the slice: x: 4, y: 4, z: 16 (z_hi: 2, z_lo: 8; z = z_hi * 8 + z_lo), core: 2. Of those that a mesh axis runs over, the one named last changes fastest.
Arguments:
- tokens: bfloat16 [16384, 8192], P('tok', 'blk'), may hold values from -6 to 6
- first_blocks: bfloat16 [64, 128, 128], P('blk'), may hold values from -0.5 to 0.5
- latter_factor_blocks: bfloat16 [64, 128, 128], P('blk'), may hold values from -0.5 to 0.5
- block_perm: int32 [64], replicated, may hold values from 0 to 63, each once
- out_grad: bfloat16 [16384, 8192], P('tok', 'blk'), may hold values from -6 to 6
Outputs:
- first_grad: float32 [64, 128, 128], P('blk', 'tok')
- latter_factor_gradient: float32 [64, 128, 128], P('blk', 'tok')
- input_grad: bfloat16 [16384, 8192], P('tok', 'blk')
Inputs may be any that keep to these rules, and one draw needn't show every extreme that they name: block_perm holds each of 0 to 63 once.
All inputs are finite; a program needn't handle non-finite values.
Results may differ from a plain program's by a relative error of at most 0.0057.
Values may be sent and summed in bfloat16 or wider, within the bound.
A program may use at most 64 MiB of HBM per device.

v0:
```python
import jax
import jax.numpy as jnp
from jax import lax
from jax.sharding import PartitionSpec as P


def gelu_value(v):
    return 0.5 * v * (1.0 + lax.erf(v * 0.7071067811865476))


def gelu_derivative(v):
    return 0.5 * (1.0 + lax.erf(v * 0.7071067811865476)) + v * 0.3989422804014327 * jnp.exp(
        -0.5 * v * v
    )


def per_device(tokens, first_blocks, latter_factor_blocks, block_perm, out_grad):
    rows = tokens.shape[0]
    local_blocks = first_blocks.shape[0]
    block_size = first_blocks.shape[1]
    combined_block_set = block_perm.shape[0]
    group = block_size // combined_block_set
    owners = lax.axis_size("blk")
    column = jnp.arange(block_size, dtype=jnp.int32)
    group_of = column // group
    group_hits = (
        group_of[:, None] == jnp.arange(combined_block_set, dtype=jnp.int32)[None, :]
    ).astype(jnp.int32)
    target = jnp.sum(group_hits * block_perm[None, :], axis=1) * group + column % group
    block_assignment = column[:, None] == target[None, :]
    placing_half = block_assignment.astype(jnp.bfloat16)
    placing_full = block_assignment.astype(jnp.float32)
    first_moved = jnp.einsum(
        "bik,jk->bij", first_blocks, placing_half, preferred_element_type=jnp.float32
    ).astype(jnp.bfloat16)
    inputs = tokens.reshape(rows, local_blocks, block_size)
    incoming_gradient = out_grad.reshape(rows, local_blocks, block_size)
    pre_cols = jnp.einsum("bio,tbi->bot", first_moved, inputs, preferred_element_type=jnp.float32)
    act_cols = gelu_value(pre_cols).astype(jnp.bfloat16)
    outgoing = act_cols.reshape(local_blocks, owners, local_blocks, group, rows).transpose(
        1, 2, 0, 3, 4
    )
    permuted_gradient = jnp.einsum(
        "vcr,lvr->vcl", latter_factor_blocks, incoming_gradient, preferred_element_type=jnp.float32
    ).astype(jnp.bfloat16)
    returning = permuted_gradient.reshape(
        local_blocks, owners, local_blocks, group, rows
    ).transpose(1, 2, 0, 3, 4)
    arrived = lax.all_to_all(outgoing, "blk", split_axis=0, concat_axis=2, tiled=True)
    came_back = lax.all_to_all(returning, "blk", split_axis=0, concat_axis=2, tiled=True)
    permuted_columns = arrived.reshape(local_blocks, block_size, rows)
    second_term = jnp.einsum(
        "qrp,pqh->qrh", permuted_columns, incoming_gradient, preferred_element_type=jnp.float32
    )
    act_grad = came_back.reshape(local_blocks, block_size, rows)
    pre_grad = (act_grad.astype(jnp.float32) * gelu_derivative(pre_cols)).astype(jnp.bfloat16)
    first_term = jnp.einsum("tbi,bjt->bij", inputs, pre_grad, preferred_element_type=jnp.float32)
    input_grad = jnp.einsum(
        "bij,bjt->tbi", first_moved, pre_grad, preferred_element_type=jnp.float32
    )
    input_grad = input_grad.astype(jnp.bfloat16).reshape(rows, local_blocks * block_size)
    latter_factor_gradient = lax.psum_scatter(second_term, "tok", scatter_dimension=1, tiled=True)
    first_moved_grad = lax.psum_scatter(first_term, "tok", scatter_dimension=1, tiled=True)
    first_grad = jnp.einsum(
        "bij,jk->bik",
        first_moved_grad,
        placing_full,
        precision=lax.Precision.HIGHEST,
        preferred_element_type=jnp.float32,
    )
    return (first_grad, latter_factor_gradient, input_grad)


def solution(mesh):
    return jax.shard_map(
        per_device,
        mesh=mesh,
        in_specs=(
            P("tok", "blk"),
            P("blk", None, None),
            P("blk", None, None),
            P(),
            P("tok", "blk"),
        ),
        out_specs=(P("blk", "tok", None), P("blk", "tok", None), P("tok", "blk")),
        check_vma=False,
    )
```

profile of v0, /device:TPU:32, one launch (start us, length us, event | category | flops | bytes accessed | tf_op | source)
XLA Modules:
  0.0 1203.1 jit_solution(10624789071451781855)
XLA Ops:
  7.2 1.5 convolution_convert_fusion.1
  8.9 1.2 copy.80
  10.1 12.8 %all-to-all-start = ((bf16[8,8,8,2,256]{4,3,1,2,0:T(2,128)(2,1)}), bf16[8,8,8,2,256]{4,3,1,2,0:T(2,128)(2,1)S(1)}, u32[]{:S(2)}, u32[]{:S(2)}) async-start(bf16[8,8,8,2,256]{4,3,1,2,0:T(2,128)(2,1)} %bitcast.58), calls=%async_computation | async-start | bytes 1048576 | tf_op jit(solution)/shard_map/all_to_all | solution.py:50
  22.9 0.6 copy-done.3
  23.9 25.8 %all-to-all-done = bf16[8,8,8,2,256]{4,3,1,2,0:T(2,128)(2,1)S(1)} async-done(((bf16[8,8,8,2,256]{4,3,1,2,0:T(2,128)(2,1)}), bf16[8,8,8,2,256]{4,3,1,2,0:T(2,128)(2,1)S(1)}, u32[]{:S(2)}, u32[]{:S(2)}) %all-to-all-start) | async-done | bytes 524320 | tf_op jit(solution)/shard_map/all_to_all | solution.py:50
  49.6 0.6 convert_bitcast_fusion
  50.2 0.6 copy.44
  50.8 0.7 reshape.64
  51.5 0.7 multiply_convert_fusion
  52.4 1.2 copy.79
  53.7 6.2 all-to-all-start.1
  59.9 0.3 convolution_bitcast_fusion
  60.2 1.0 copy.47
  61.2 25.1 %all-to-all-done.1 = bf16[8,8,8,2,256]{4,3,1,2,0:T(2,128)(2,1)S(1)} async-done(((bf16[8,8,8,2,256]{4,3,1,2,0:T(2,128)(2,1)}), bf16[8,8,8,2,256]{4,3,1,2,0:T(2,128)(2,1)S(1)}, u32[]{:S(2)}, u32[]{:S(2)}) %all-to-all-start.1) | async-done | bytes 524320 | tf_op jit(solution)/shard_map/all_to_all | solution.py:49
  86.3 0.4 copy.49
  86.9 0.8 copy-done.1
  88.1 1.1 copy.51
  89.2 0.3 convolution_convert_fusion
  89.5 1.0 copy.55
  90.5 542.8 %reduce-scatter.3.cloned.1.call-done = f32[8,2,128]{2,0,1:T(8,128)} async-done(((f32[8,128,128]{2,0,1:T(8,128)}), f32[8,2,128]{2,0,1:T(8,128)}) %reduce-scatter.3.cloned.1.call-update) | async-done | bytes 8208 | tf_op jit(solution)/shard_map/reduce_scatter | solution.py:63
  633.3 0.8 fusion.17
  634.1 0.6 copy.53
  634.8 560.2 %reduce-scatter.5.cloned.1.call-done = f32[8,2,128]{2,0,1:T(8,128)} async-done(((f32[8,128,128]{2,0,1:T(8,128)}), f32[8,2,128]{2,0,1:T(8,128)}) %reduce-scatter.5.cloned.1.call-update) | async-done | bytes 8208 | tf_op jit(solution)/shard_map/reduce_scatter | solution.py:62
  1195.0 1.3 copy.54
  (18 shorter events, 1.3 us)
Async XLA Ops:
  7.2 44.4 %copy-start = (bf16[256,1024]{1,0:T(8,128)(2,1)S(1)}, bf16[256,1024]{1,0:T(8,128)(2,1)}, u32[]{:S(2)}) copy-start(bf16[256,1024]{1,0:T(8,128)(2,1)} %param.5) | copy-start | bytes 1572868
  10.1 13.5 %copy-start.2 = (bf16[8,128,128]{2,1,0:T(8,128)(2,1)S(1)}, bf16[8,128,128]{2,1,0:T(8,128)(2,1)}, u32[]{:S(2)}) copy-start(bf16[8,128,128]{2,1,0:T(8,128)(2,1)} %param.6) | copy-start | bytes 786436
  10.1 39.5 %all-to-all-start = ((bf16[8,8,8,2,256]{4,3,1,2,0:T(2,128)(2,1)}), bf16[8,8,8,2,256]{4,3,1,2,0:T(2,128)(2,1)S(1)}, u32[]{:S(2)}, u32[]{:S(2)}) async-start(bf16[8,8,8,2,256]{4,3,1,2,0:T(2,128)(2,1)} %bitcast.58), calls=%async_computation | async-start | bytes 1048576 | tf_op jit(solution)/shard_map/all_to_all | solution.py:50
  22.9 0.7 copy-start.3
  53.7 32.7 %all-to-all-start.1 = ((bf16[8,8,8,2,256]{4,3,1,2,0:T(2,128)(2,1)}), bf16[8,8,8,2,256]{4,3,1,2,0:T(2,128)(2,1)S(1)}, u32[]{:S(2)}, u32[]{:S(2)}) async-start(bf16[8,8,8,2,256]{4,3,1,2,0:T(2,128)(2,1)} %bitcast.57), calls=%async_computation.2 | async-start | bytes 1048576 | tf_op jit(solution)/shard_map/all_to_all | solution.py:49
  59.9 573.4 %reduce-scatter.3.cloned.1.call-start = ((), (), s32[]{:S(2)}) async-start(), calls=%async_computation.4 | async-start | bytes 532480 | tf_op jit(solution)/shard_map/reduce_scatter | solution.py:63
  61.2 1133.8 %reduce-scatter.5.cloned.1.call-start = ((), (), s32[]{:S(2)}) async-start(), calls=%async_computation.5 | async-start | bytes 532480 | tf_op jit(solution)/shard_map/reduce_scatter | solution.py:62
  86.7 1.0 copy-start.1
Sparse Core Ops, SparseCore 0:
  63.5 569.7 reduce-scatter.2
  636.3 558.6 reduce-scatter.4
where the time goes:
time: 1200 us
  waiting for transfers between devices  1150 us (96%)
  starting transfers between devices  19 us (2%)
  between operations  14.2 us (1%)
    reduce_scatter x1, waiting for transfers between devices, per_device(): lax.psum_scatter(second_term, 'tok', scatter_dimension=1, tiled=True)  560 us
    reduce_scatter x1, waiting for transfers between devices, per_device(): lax.psum_scatter(first_term, 'tok', scatter_dimension=1, tiled=True)  543 us
    all_to_all x1, waiting for transfers between devices, per_device(): lax.all_to_all(returning, 'blk', split_axis=0, concat_axis=2, tiled=True)  25.8 us
    all_to_all x1, waiting for transfers between devices, per_device(): lax.all_to_all(outgoing, 'blk', split_axis=0, concat_axis=2, tiled=True)  25.1 us
  transfers between devices with their start and end apart: 4, of which 4 were waited for; matrix products, arithmetic and copies ran while one was open for 1% of the time, Pallas kernels for 0%

commit v1 on v0

v1 whole, which is shorter than its diff:
```python
import jax
import jax.numpy as jnp
from jax import lax
from jax.experimental import pallas as pl
from jax.experimental.pallas import tpu as pltpu
from jax.sharding import PartitionSpec as P

MESH = pl.DeviceIdType.MESH
F32 = jnp.float32
BF16 = jnp.bfloat16
ROWS = 256
BS = 128
NBL = 8


def dot_nn(a, b):
    return lax.dot_general(a, b, (((1,), (0,)), ((), ())), preferred_element_type=F32)


def dot_nt(a, b):
    return lax.dot_general(a, b, (((1,), (1,)), ((), ())), preferred_element_type=F32)


def dot_tn(a, b):
    return lax.dot_general(a, b, (((0,), (0,)), ((), ())), preferred_element_type=F32)


def iota(dim):
    return lax.broadcasted_iota(jnp.int32, (BS, BS), dim)


def one_hot(hit):
    return jnp.where(hit, 1.0, 0.0).astype(BF16)


def kernel(
    x_ref, w_ref, l_ref, perm_ref, og_ref,
    fg_ref, lg_ref, ig_ref,
    wm, tmp, dgelu, send_mg, recv_mg, send_act, recv_act,
    g_all, r_core, s_core, r_y, s_y, r_x, s_x, r_z,
    a2a_send, a2a_recv, rs_send, rs_recv,
):
    b = lax.axis_index("blk")
    t = lax.axis_index("tok")
    zh, x, y, core = t // 32, (t // 8) % 4, (t // 2) % 4, t % 2
    half, place = b // 4, b % 4

    def ring(at, k):
        return (at + k) % 4

    core_peer = (b, t + 1 - 2 * core)
    zh_peer = (b, t + 32 - 64 * zh)

    def y_peer(k):
        return (b, t + (ring(y, k) - y) * 2)

    def x_peer(k):
        return (b, t + (ring(x, k) - x) * 8)

    far = [(1 - half) * 4 + ring(place, k) for k in range(4)]
    near = [half * 4 + ring(place, k) for k in range(1, 4)]
    others = far + near

    barrier = pltpu.get_barrier_semaphore()
    peers = [(s, t) for s in others] + [core_peer, zh_peer]
    peers += [y_peer(k) for k in range(1, 4)] + [x_peer(k) for k in range(1, 4)]
    for peer in peers:
        pl.semaphore_signal(barrier, inc=1, device_id=peer, device_id_type=MESH)

    row, col = iota(0), iota(1)
    swap = one_hot(col == ((row >> 1) & 7) * 16 + (row >> 4) * 2 + (row & 1))
    by_core = one_hot(
        col
        == ((row >> 3) & 1) * 64
        + ((row >> 1) & 3) * 16
        + ((row >> 4) & 3) * 4
        + (row >> 6) * 2
        + (row & 1)
    )

    def slab(s):
        return pl.ds(pl.multiple_of(s * 16, 16), 16)

    def a2a(phase, s, send, recv):
        return pltpu.make_async_remote_copy(
            src_ref=send.at[s],
            dst_ref=recv.at[:, slab(b), :],
            send_sem=a2a_send.at[phase, s],
            recv_sem=a2a_recv.at[phase, b],
            device_id=(s, t),
            device_id_type=MESH,
        )

    def landed(phase, s, send, recv):
        return pltpu.make_async_remote_copy(
            src_ref=send.at[s],
            dst_ref=recv.at[:, slab(s), :],
            send_sem=a2a_send.at[phase, s],
            recv_sem=a2a_recv.at[phase, s],
            device_id=(s, t),
            device_id_type=MESH,
        )

    def swapped(s):
        chunk = tmp[:, slab(s), :].reshape(BS, ROWS)
        return dot_nn(swap, chunk).astype(BF16).reshape(NBL, 16, ROWS)

    for d in range(NBL):
        cols = slice(d * BS, (d + 1) * BS)
        tmp[d] = dot_nt(l_ref[d], og_ref[:, cols]).astype(BF16)
    for at, s in enumerate(others):
        send_mg[s] = swapped(s)
        if at == 0:
            pl.semaphore_wait(barrier, len(peers))
        a2a(0, s, send_mg, recv_mg).start()
    recv_mg[:, slab(b), :] = swapped(b)

    perm = jnp.broadcast_to(perm_ref[...].astype(F32), (16, 64)).astype(BF16)
    pair = one_hot(iota(1)[:64] // 2 == iota(0)[:64])
    target = dot_nn(perm, pair)[:1] * 2.0 + (iota(1)[:1] % 2).astype(F32)
    placing = one_hot(iota(0).astype(F32) == target)
    for a in range(NBL):
        cols = slice(a * BS, (a + 1) * BS)
        wm[a] = dot_nt(placing, w_ref[a]).astype(BF16)
        pre = dot_nt(wm[a], x_ref[:, cols])
        cdf = 0.5 * (1.0 + lax.erf(pre * 0.7071067811865476))
        tmp[a] = (pre * cdf).astype(BF16)
        dgelu[a] = cdf + pre * 0.3989422804014327 * jnp.exp(-0.5 * pre * pre)
    for s in others:
        send_act[s] = swapped(s)
        a2a(1, s, send_act, recv_act).start()
    recv_act[:, slab(b), :] = swapped(b)

    def copy(g, at_src, at_dst, src, dst, peer):
        return pltpu.make_async_remote_copy(
            src_ref=src,
            dst_ref=dst,
            send_sem=rs_send.at[g, at_src],
            recv_sem=rs_recv.at[g, at_dst],
            device_id=peer,
            device_id_type=MESH,
        )

    def core_half(c):
        return pl.ds(pl.multiple_of(c * 64, 64), 64)

    def scatter_sum(g, out_ref):
        sends = []
        copies = copy(
            g, 0, 0, g_all.at[g, :, core_half(1 - core), :], r_core.at[g], core_peer
        )
        copies.start()
        copies.wait_recv()
        sends.append(copies)
        s_core[g] = (
            g_all[g, :, core_half(core), :].astype(F32) + r_core[g].astype(F32)
        ).astype(BF16)
        for k in range(1, 4):
            to = ring(y, k)
            c = copy(
                g, 1 + to, 1 + y, s_core.at[g, :, slab(to), :], r_y.at[g, y], y_peer(k)
            )
            c.start()
            sends.append(c)
        total = s_core[g, :, slab(y), :].astype(F32)
        for k in range(1, 4):
            at = ring(y, k)
            copy(
                g, 1 + at, 1 + at, s_core.at[g, :, slab(at), :], r_y.at[g, at], y_peer(k)
            ).wait_recv()
            total = total + r_y[g, at].astype(F32)
        s_y[g] = (
            dot_nn(swap, total.astype(BF16).reshape(BS, BS))
            .astype(BF16)
            .reshape(2, 4, 16, BS)
        )
        for k in range(1, 4):
            to = ring(x, k)
            c = copy(g, 5 + to, 5 + x, s_y.at[g, :, to], r_x.at[g, x], x_peer(k))
            c.start()
            sends.append(c)
        total = s_y[g, :, x].astype(F32)
        for k in range(1, 4):
            at = ring(x, k)
            copy(
                g, 5 + at, 5 + at, s_y.at[g, :, at], r_x.at[g, at], x_peer(k)
            ).wait_recv()
            total = total + r_x[g, at].astype(F32)
        s_x[g] = total
        c = copy(g, 9, 9, s_x.at[g, 1 - zh], r_z.at[g], zh_peer)
        c.start()
        c.wait_recv()
        sends.append(c)
        total = s_x[g, zh] + r_z[g]
        for a in range(NBL):
            out_ref[a] = total[2 * a : 2 * a + 2]
        return sends

    for s in others:
        landed(0, s, send_mg, recv_mg).wait_recv()
    for a in range(NBL):
        cols = slice(a * BS, (a + 1) * BS)
        pg = (recv_mg[a].astype(F32) * dgelu[a]).astype(BF16)
        grad = dot_nn(pg, x_ref[:, cols]).astype(BF16)
        moved = dot_nt(by_core, grad).astype(BF16)
        g_all[0, a] = dot_nn(moved, placing).astype(BF16)
        ig_ref[:, cols] = dot_tn(pg, wm[a]).astype(BF16)
    sends = scatter_sum(0, fg_ref)

    for s in others:
        landed(1, s, send_act, recv_act).wait_recv()
    for d in range(NBL):
        cols = slice(d * BS, (d + 1) * BS)
        grad = dot_nn(recv_act[d], og_ref[:, cols]).astype(BF16)
        g_all[1, d] = dot_nn(by_core, grad).astype(BF16)
    sends += scatter_sum(1, lg_ref)

    for s in others:
        a2a(0, s, send_mg, recv_mg).wait_send()
        a2a(1, s, send_act, recv_act).wait_send()
    for c in sends:
        c.wait_send()


def per_device(tokens, first_blocks, latter_factor_blocks, block_perm, out_grad):
    vmem = pl.BlockSpec(memory_space=pltpu.VMEM)
    return pl.pallas_call(
        kernel,
        out_shape=(
            jax.ShapeDtypeStruct((NBL, 2, BS), F32),
            jax.ShapeDtypeStruct((NBL, 2, BS), F32),
            jax.ShapeDtypeStruct((ROWS, NBL * BS), BF16),
        ),
        in_specs=[vmem] * 5,
        out_specs=[vmem] * 3,
        scratch_shapes=[
            pltpu.VMEM((NBL, BS, BS), BF16),
            pltpu.VMEM((NBL, BS, ROWS), BF16),
            pltpu.VMEM((NBL, BS, ROWS), F32),
            pltpu.VMEM((NBL, NBL, 16, ROWS), BF16),
            pltpu.VMEM((NBL, BS, ROWS), BF16),
            pltpu.VMEM((NBL, NBL, 16, ROWS), BF16),
            pltpu.VMEM((NBL, BS, ROWS), BF16),
            pltpu.VMEM((2, NBL, BS, BS), BF16),
            pltpu.VMEM((2, NBL, 64, BS), BF16),
            pltpu.VMEM((2, NBL, 64, BS), BF16),
            pltpu.VMEM((2, 4, NBL, 16, BS), BF16),
            pltpu.VMEM((2, 2, 4, 16, BS), BF16),
            pltpu.VMEM((2, 4, 2, 16, BS), BF16),
            pltpu.VMEM((2, 2, 16, BS), F32),
            pltpu.VMEM((2, 16, BS), F32),
            pltpu.SemaphoreType.DMA((2, NBL)),
            pltpu.SemaphoreType.DMA((2, NBL)),
            pltpu.SemaphoreType.DMA((2, 10)),
            pltpu.SemaphoreType.DMA((2, 10)),
        ],
        compiler_params=pltpu.CompilerParams(
            collective_id=0, has_side_effects=True, vmem_limit_bytes=48 * 2**20
        ),
    )(tokens, first_blocks, latter_factor_blocks, block_perm.reshape(1, 64), out_grad)


def solution(mesh):
    return jax.shard_map(
        per_device,
        mesh=mesh,
        in_specs=(
            P("tok", "blk"),
            P("blk", None, None),
            P("blk", None, None),
            P(),
            P("tok", "blk"),
        ),
        out_specs=(P("blk", "tok", None), P("blk", "tok", None), P("tok", "blk")),
        check_vma=False,
    )
```

time: 1200 us -> 95.5 us (0.08)
  the two profiles are of different devices: /device:TPU:32 before, /device:TPU:1 now
where the time goes in v1:
time: 95.5 us; the launch traced here: 95.2 us
  Pallas kernels  88 us (92%)
  local copies, waits for them, and re-layouts  6.62 us (7%)
    pallas_call x1, Pallas kernels, per_device(): pl.pallas_call(kernel, out_shape=(jax.ShapeDtypeStruct((NBL, 2, BS), F32)...  88 us
    unnamed x13, local copies, waits for them, and re-layouts  6.62 us

profile of v1, /device:TPU:1, one launch (start us, length us, event | category | flops | bytes accessed | tf_op | source)
XLA Modules:
  0.0 95.2 jit_solution(18229372579708925527)
XLA Ops:
  0.6 0.0 copy-start.4
  0.6 0.6 copy-done.4
  1.3 0.0 copy-start
  1.3 1.0 %copy-done = bf16[256,1024]{1,0:T(8,128)(2,1)S(1)} copy-done((bf16[256,1024]{1,0:T(8,128)(2,1)S(1)}, bf16[256,1024]{1,0:T(8,128)(2,1)}, u32[]{:S(2)}) %copy-start) | copy-done | bytes 524312
  2.3 0.0 copy-start.1
  2.3 1.0 %copy-done.1 = bf16[256,1024]{1,0:T(8,128)(2,1)S(1)} copy-done((bf16[256,1024]{1,0:T(8,128)(2,1)S(1)}, bf16[256,1024]{1,0:T(8,128)(2,1)}, u32[]{:S(2)}) %copy-start.1) | copy-done | bytes 524312
  3.4 0.0 copy-start.2
  3.4 0.9 copy-done.2
  4.3 0.0 copy-start.3
  4.3 0.9 copy-done.3
  5.3 88.0 %shard_map.76 = (f32[8,2,128]{2,1,0:T(2,128)S(1)}, f32[8,2,128]{2,1,0:T(2,128)S(1)}, bf16[256,1024]{1,0:T(8,128)(2,1)S(1)}) custom-call(bf16[256,1024]{1,0:T(8,128)(2,1)S(1)} %copy-done, bf16[8,128,128]{2,1,0:T(8,128)(2,1)S(1)} %copy-done.2, bf16[8,128,128]{2,1,0:T(8,128)(2,1)S(1)} %copy-done.3, s32[1,64]{1,0:T(1,128)S(1)} %bitcast.1, ...), custom_call_target="tpu_custom_call" | custom-call | tf_op jit(solution)/shard_map/pallas_call | solution.py:227
  93.2 0.6 copy.11
  93.8 0.6 copy.12
  94.4 0.8 copy.13
Async XLA Ops:
  0.6 0.7 copy-start.4
  1.3 1.0 %copy-start = (bf16[256,1024]{1,0:T(8,128)(2,1)S(1)}, bf16[256,1024]{1,0:T(8,128)(2,1)}, u32[]{:S(2)}) copy-start(bf16[256,1024]{1,0:T(8,128)(2,1)} %x_ref.1) | copy-start | bytes 1572868
  2.3 1.0 %copy-start.1 = (bf16[256,1024]{1,0:T(8,128)(2,1)S(1)}, bf16[256,1024]{1,0:T(8,128)(2,1)}, u32[]{:S(2)}) copy-start(bf16[256,1024]{1,0:T(8,128)(2,1)} %og_ref.1) | copy-start | bytes 1572868
  3.4 0.9 copy-start.2
  4.3 0.9 copy-start.3

commit v2 on v1

v2 whole, which is shorter than its diff:
```python
import jax
import jax.numpy as jnp
from jax import lax
from jax.experimental import pallas as pl
from jax.experimental.pallas import tpu as pltpu
from jax.sharding import PartitionSpec as P

MESH = pl.DeviceIdType.MESH
F32 = jnp.float32
BF16 = jnp.bfloat16
ROWS = 256
BS = 128
NBL = 8
HOLD = True


def dot_nn(a, b):
    return lax.dot_general(a, b, (((1,), (0,)), ((), ())), preferred_element_type=F32)


def dot_nt(a, b):
    return lax.dot_general(a, b, (((1,), (1,)), ((), ())), preferred_element_type=F32)


def dot_tn(a, b):
    return lax.dot_general(a, b, (((0,), (0,)), ((), ())), preferred_element_type=F32)


def iota(dim):
    return lax.broadcasted_iota(jnp.int32, (BS, BS), dim)


def one_hot(hit):
    return jnp.where(hit, 1.0, 0.0).astype(BF16)


def kernel(
    x_hbm, w_hbm, l_hbm, perm_hbm, og_hbm,
    fg_ref, lg_ref, ig_ref,
    x_ref, w_ref, l_ref, perm_ref, og_ref, in_sem,
    wm, tmp, dgelu, send_mg, recv_mg, send_act, recv_act, part,
    g_core, r_core, s_core, r_y, s_y, r_x, s_x, r_z,
    a2a_send, a2a_recv, rs_send, rs_recv, edge_sem, open_sem,
):
    b = lax.axis_index("blk")
    t = lax.axis_index("tok")
    zh, x, y, core = t // 32, (t // 8) % 4, (t // 2) % 4, t % 2
    half, place = b // 4, b % 4

    def ring(at, k):
        return (at + k) % 4

    core_peer = (b, t + 1 - 2 * core)
    zh_peer = (b, t + 32 - 64 * zh)

    def y_peer(k):
        return (b, t + (ring(y, k) - y) * 2)

    def x_peer(k):
        return (b, t + (ring(x, k) - x) * 8)

    far = [(1 - half) * 4 + ring(place, k) for k in range(4)]
    near = [half * 4 + ring(place, k) for k in range(1, 4)]
    others = far + near

    at_edge = b == 7 - 7 * zh
    edge_peer = (7 - b, t + 32 - 64 * zh)

    def signal(sem, peer):
        pl.semaphore_signal(sem, inc=1, device_id=peer, device_id_type=MESH)

    barrier = pltpu.get_barrier_semaphore()
    peers = [(s, t) for s in others] + [core_peer]
    peers += [y_peer(k) for k in range(1, 4)] + [x_peer(k) for k in range(1, 4)]
    for peer in peers:
        signal(barrier, peer)

    @pl.when(at_edge)
    def _():
        signal(barrier, edge_peer)

    loads = [
        pltpu.make_async_copy(src, dst, in_sem.at[i])
        for i, (src, dst) in enumerate(
            (
                (og_hbm, og_ref),
                (l_hbm, l_ref),
                (w_hbm, w_ref),
                (x_hbm, x_ref),
                (perm_hbm, perm_ref),
            )
        )
    ]
    for load in loads:
        load.start()

    row, col = iota(0), iota(1)
    swap = one_hot(col == ((row >> 1) & 7) * 16 + (row >> 4) * 2 + (row & 1))

    def slab(s):
        return pl.ds(pl.multiple_of(s * 16, 16), 16)

    def a2a(phase, to, at, send, recv):
        return pltpu.make_async_remote_copy(
            src_ref=send.at[to],
            dst_ref=recv.at[:, slab(at), :],
            send_sem=a2a_send.at[phase, to],
            recv_sem=a2a_recv.at[phase, at],
            device_id=(to, t),
            device_id_type=MESH,
        )

    def mg_copy(to, at):
        return a2a(0, to, at, send_mg, recv_mg)

    def act_copy(to, at):
        return a2a(1, to, at, send_act, recv_act)

    def swapped(src, s):
        width = src.shape[-1]
        chunk = src[:, slab(s), :].reshape(BS, width)
        return dot_nn(swap, chunk).astype(BF16).reshape(NBL, 16, width)

    loads[0].wait()
    loads[1].wait()
    for d in range(NBL):
        cols = slice(d * BS, (d + 1) * BS)
        tmp[d] = dot_nt(l_ref[d], og_ref[:, cols]).astype(BF16)
    for at, s in enumerate(others):
        send_mg[s] = swapped(tmp, s)
        if at == 0:
            pl.semaphore_wait(barrier, len(peers) + jnp.where(at_edge, 1, 0))
        mg_copy(s, b).start()
    recv_mg[:, slab(b), :] = swapped(tmp, b)

    @pl.when(at_edge)
    def _():
        signal(edge_sem, edge_peer)

    for load in loads[2:]:
        load.wait()
    perm = jnp.broadcast_to(perm_ref[...].astype(F32), (16, 64)).astype(BF16)
    pair = one_hot(iota(1)[:64] // 2 == iota(0)[:64])
    target = dot_nn(perm, pair)[:1] * 2.0 + (iota(1)[:1] % 2).astype(F32)
    placing = one_hot(iota(0).astype(F32) == target)
    for a in range(NBL):
        cols = slice(a * BS, (a + 1) * BS)
        wm[a] = dot_nt(placing, w_ref[a]).astype(BF16)
        pre = dot_nt(wm[a], x_ref[:, cols])
        cdf = 0.5 * (1.0 + lax.erf(pre * 0.7071067811865476))
        tmp[a] = (pre * cdf).astype(BF16)
        dgelu[a] = cdf + pre * 0.3989422804014327 * jnp.exp(-0.5 * pre * pre)
    for s in near + far:
        send_act[s] = swapped(tmp, s)
    recv_act[:, slab(b), :] = swapped(tmp, b)
    for s in near:
        act_copy(s, b).start()
    for s in far:
        if HOLD:
            mg_copy(s, b).wait_send()
        act_copy(s, b).start()

    @pl.when(at_edge)
    def _():
        pl.semaphore_wait(edge_sem, 1)
        for k in range(1, 8):
            signal(open_sem, ((b + k) % 8, t))

    @pl.when(jnp.logical_not(at_edge))
    def _():
        pl.semaphore_wait(open_sem, 1)

    sends = []

    def copy(n, at_src, at_dst, src, dst, peer):
        return pltpu.make_async_remote_copy(
            src_ref=src,
            dst_ref=dst,
            send_sem=rs_send.at[n, at_src],
            recv_sem=rs_recv.at[n, at_dst],
            device_id=peer,
            device_id_type=MESH,
        )

    def plane_sum(n):
        c = copy(n, 0, 0, g_core.at[n, :, :, 1 - core], r_core.at[n], core_peer)
        c.start()
        c.wait_recv()
        sends.append(c)
        s_core[n] = (g_core[n, :, :, core].astype(F32) + r_core[n].astype(F32)).astype(
            BF16
        )
        for k in range(1, 4):
            to = ring(y, k)
            c = copy(n, 1 + to, 1 + y, s_core.at[n, :, to], r_y.at[n, y], y_peer(k))
            c.start()
            sends.append(c)
        total = s_core[n, :, y].astype(F32)
        for k in range(1, 4):
            at = ring(y, k)
            copy(
                n, 1 + at, 1 + at, s_core.at[n, :, at], r_y.at[n, at], y_peer(k)
            ).wait_recv()
            total = total + r_y[n, at].astype(F32)
        s_y[n] = total.astype(BF16)
        for k in range(1, 4):
            to = ring(x, k)
            c = copy(n, 5 + to, 5 + x, s_y.at[n, to], r_x.at[n, x], x_peer(k))
            c.start()
            sends.append(c)
        total = s_y[n, x].astype(F32)
        for k in range(1, 4):
            at = ring(x, k)
            copy(
                n, 5 + at, 5 + at, s_y.at[n, at], r_x.at[n, at], x_peer(k)
            ).wait_recv()
            total = total + r_x[n, at].astype(F32)
        return total

    def across(g):
        return copy(2 * g, 9, 9, s_x.at[g, 1 - zh], r_z.at[g], zh_peer)

    def finish(g, out_ref):
        across(g).wait_recv()
        total = s_x[g, zh] + r_z[g]
        for a in range(NBL):
            out_ref[a] = total[2 * a : 2 * a + 2]

    for s in others:
        mg_copy(s, s).wait_recv()
    for a in range(NBL):
        cols = slice(a * BS, (a + 1) * BS)
        pg = (recv_mg[a].astype(F32) * dgelu[a]).astype(BF16)
        grad = dot_nn(pg, x_ref[:, cols]).astype(BF16)
        part[a] = dot_tn(grad, placing).astype(BF16)
        ig_ref[:, cols] = dot_tn(pg, wm[a]).astype(BF16)
    for s in range(NBL):
        g_core[s // 4, s % 4] = swapped(part, s).reshape(4, 2, 16, BS)
    s_x[0, 0] = plane_sum(0)
    s_x[0, 1] = plane_sum(1)
    across(0).start()

    def second(which, sources, h):
        for s in sources:
            act_copy(s, s).wait_recv()
        rows = pl.ds(pl.multiple_of(h * 64, 64), 64)
        for d in range(NBL):
            cols = slice(d * BS, (d + 1) * BS)
            part[d, :64] = dot_nn(recv_act[d, rows, :], og_ref[:, cols]).astype(BF16)
        for s in range(4):
            g_core[which, s] = swapped(part, s).reshape(4, 2, 16, BS)
        s_x[1, h] = plane_sum(which)

    second(2, near, half)

    @pl.when(zh != half)
    def _():
        across(1).start()

    second(3, far, 1 - half)

    @pl.when(zh == half)
    def _():
        across(1).start()

    finish(0, fg_ref)
    finish(1, lg_ref)
    for s in others:
        if not HOLD:
            mg_copy(s, b).wait_send()
        act_copy(s, b).wait_send()
    if HOLD:
        for s in near:
            mg_copy(s, b).wait_send()
    for c in sends:
        c.wait_send()
    across(0).wait_send()
    across(1).wait_send()


def per_device(tokens, first_blocks, latter_factor_blocks, block_perm, out_grad):
    vmem = pl.BlockSpec(memory_space=pltpu.VMEM)
    hbm = pl.BlockSpec(memory_space=pltpu.HBM)
    return pl.pallas_call(
        kernel,
        out_shape=(
            jax.ShapeDtypeStruct((NBL, 2, BS), F32),
            jax.ShapeDtypeStruct((NBL, 2, BS), F32),
            jax.ShapeDtypeStruct((ROWS, NBL * BS), BF16),
        ),
        in_specs=[hbm] * 5,
        out_specs=[vmem] * 3,
        scratch_shapes=[
            pltpu.VMEM((ROWS, NBL * BS), BF16),
            pltpu.VMEM((NBL, BS, BS), BF16),
            pltpu.VMEM((NBL, BS, BS), BF16),
            pltpu.VMEM((1, 64), jnp.int32),
            pltpu.VMEM((ROWS, NBL * BS), BF16),
            pltpu.SemaphoreType.DMA((5,)),
            pltpu.VMEM((NBL, BS, BS), BF16),
            pltpu.VMEM((NBL, BS, ROWS), BF16),
            pltpu.VMEM((NBL, BS, ROWS), F32),
            pltpu.VMEM((NBL, NBL, 16, ROWS), BF16),
            pltpu.VMEM((NBL, BS, ROWS), BF16),
            pltpu.VMEM((NBL, NBL, 16, ROWS), BF16),
            pltpu.VMEM((NBL, BS, ROWS), BF16),
            pltpu.VMEM((NBL, BS, BS), BF16),
            pltpu.VMEM((4, 4, 4, 2, 16, BS), BF16),
            pltpu.VMEM((4, 4, 4, 16, BS), BF16),
            pltpu.VMEM((4, 4, 4, 16, BS), BF16),
            pltpu.VMEM((4, 4, 4, 16, BS), BF16),
            pltpu.VMEM((4, 4, 16, BS), BF16),
            pltpu.VMEM((4, 4, 16, BS), BF16),
            pltpu.VMEM((2, 2, 16, BS), F32),
            pltpu.VMEM((2, 16, BS), F32),
            pltpu.SemaphoreType.DMA((2, NBL)),
            pltpu.SemaphoreType.DMA((2, NBL)),
            pltpu.SemaphoreType.DMA((4, 10)),
            pltpu.SemaphoreType.DMA((4, 10)),
            pltpu.SemaphoreType.REGULAR,
            pltpu.SemaphoreType.REGULAR,
        ],
        compiler_params=pltpu.CompilerParams(
            collective_id=0, has_side_effects=True, vmem_limit_bytes=56 * 2**20
        ),
    )(tokens, first_blocks, latter_factor_blocks, block_perm.reshape(1, 64), out_grad)


def solution(mesh):
    return jax.shard_map(
        per_device,
        mesh=mesh,
        in_specs=(
            P("tok", "blk"),
            P("blk", None, None),
            P("blk", None, None),
            P(),
            P("tok", "blk"),
        ),
        out_specs=(P("blk", "tok", None), P("blk", "tok", None), P("tok", "blk")),
        check_vma=False,
    )
```

time: 95.5 us -> 94.3 us (0.987)
  the two profiles are of different devices: /device:TPU:1 before, /device:TPU:128 now
where the time goes in v2:
time: 94.3 us; the launch traced here: 94 us
  Pallas kernels  89.6 us (95%)
  local copies, waits for them, and re-layouts  3.77 us (4%)
    pallas_call x1, Pallas kernels, per_device(): pl.pallas_call(kernel, out_shape=(jax.ShapeDtypeStruct((NBL, 2, BS), F32)...  89.6 us
    unnamed x5, local copies, waits for them, and re-layouts  3.77 us

profile of v2, /device:TPU:128, one launch (start us, length us, event | category | flops | bytes accessed | tf_op | source)
XLA Modules:
  0.0 94.0 jit_solution(13603647045401202967)
XLA Ops:
  0.6 89.6 %shard_map.76 = (f32[8,2,128]{2,1,0:T(2,128)}, f32[8,2,128]{2,1,0:T(2,128)}, bf16[256,1024]{1,0:T(8,128)(2,1)}) custom-call(bf16[256,1024]{1,0:T(8,128)(2,1)} %x_hbm.1, bf16[8,128,128]{2,1,0:T(8,128)(2,1)} %w_hbm.1, bf16[8,128,128]{2,1,0:T(8,128)(2,1)} %l_hbm.1, s32[1,64]{1,0:T(1,128)} %bitcast.1, bf16[256,1024]{1,0:T(8,128)(2,1)} %og_hbm.1), custom_call_target="tpu_custom_call" | custom-call | tf_op jit(solution)/shard_map/pallas_call | solution.py:284
  90.2 0.0 copy-start
  90.3 1.3 %copy.11 = f32[8,2,128]{2,1,0:T(2,128)} copy(f32[8,2,128]{2,1,0:T(2,128)} %get-tuple-element.6) | data formatting | bytes 16384
  91.6 0.0 copy-done
  91.6 0.6 copy.12
  92.2 1.9 %copy.13 = bf16[256,1024]{1,0:T(8,128)(2,1)} copy(bf16[256,1024]{1,0:T(8,128)(2,1)} %get-tuple-element.8) | data formatting | bytes 1048576
Async XLA Ops:
  90.2 1.3 %copy-start = (f32[8,2,128]{2,1,0:T(2,128)S(1)}, f32[8,2,128]{2,1,0:T(2,128)}, u32[]{:S(2)}) copy-start(f32[8,2,128]{2,1,0:T(2,128)} %get-tuple-element.7) | copy-start | bytes 24580

commit v3 on v2

--- a/solution.py
+++ b/solution.py
@@ -39,22 +39,21 @@
     fg_ref, lg_ref, ig_ref,
     x_ref, w_ref, l_ref, perm_ref, og_ref, in_sem,
     wm, tmp, dgelu, send_mg, recv_mg, send_act, recv_act, part,
-    g_core, r_core, s_core, r_y, s_y, r_x, s_x, r_z,
+    g_early, rq_early, sq_early, rx_early, g_late, rq_late, sq_late, rx_late, s_x, r_z,
     a2a_send, a2a_recv, rs_send, rs_recv, edge_sem, open_sem,
 ):
     b = lax.axis_index("blk")
     t = lax.axis_index("tok")
-    zh, x, y, core = t // 32, (t // 8) % 4, (t // 2) % 4, t % 2
+    zh, x, q = t // 32, (t // 8) % 4, t % 8
     half, place = b // 4, b % 4
 
     def ring(at, k):
         return (at + k) % 4
 
-    core_peer = (b, t + 1 - 2 * core)
     zh_peer = (b, t + 32 - 64 * zh)
 
-    def y_peer(k):
-        return (b, t + (ring(y, k) - y) * 2)
+    def q_peer(k):
+        return (b, t + (q + k) % 8 - q)
 
     def x_peer(k):
         return (b, t + (ring(x, k) - x) * 8)
@@ -70,8 +69,8 @@
         pl.semaphore_signal(sem, inc=1, device_id=peer, device_id_type=MESH)
 
     barrier = pltpu.get_barrier_semaphore()
-    peers = [(s, t) for s in others] + [core_peer]
-    peers += [y_peer(k) for k in range(1, 4)] + [x_peer(k) for k in range(1, 4)]
+    peers = [(s, t) for s in others]
+    peers += [q_peer(k) for k in range(1, 8)] + [x_peer(k) for k in range(1, 4)]
     for peer in peers:
         signal(barrier, peer)
 
@@ -182,43 +181,32 @@
             device_id_type=MESH,
         )
 
-    def plane_sum(n):
-        c = copy(n, 0, 0, g_core.at[n, :, :, 1 - core], r_core.at[n], core_peer)
-        c.start()
-        c.wait_recv()
-        sends.append(c)
-        s_core[n] = (g_core[n, :, :, core].astype(F32) + r_core[n].astype(F32)).astype(
-            BF16
-        )
-        for k in range(1, 4):
-            to = ring(y, k)
-            c = copy(n, 1 + to, 1 + y, s_core.at[n, :, to], r_y.at[n, y], y_peer(k))
+    def plane_sum(n, g, r_q, s_q, r_x):
+        for k in range(1, 8):
+            to = (q + k) % 8
+            c = copy(n, to, q, g.at[:, :, to], r_q.at[q], q_peer(k))
             c.start()
             sends.append(c)
-        total = s_core[n, :, y].astype(F32)
-        for k in range(1, 4):
-            at = ring(y, k)
-            copy(
-                n, 1 + at, 1 + at, s_core.at[n, :, at], r_y.at[n, at], y_peer(k)
-            ).wait_recv()
-            total = total + r_y[n, at].astype(F32)
-        s_y[n] = total.astype(BF16)
+        total = g[:, :, q].astype(F32)
+        for k in range(1, 8):
+            at = (q + k) % 8
+            copy(n, at, at, g.at[:, :, at], r_q.at[at], q_peer(k)).wait_recv()
+            total = total + r_q[at].astype(F32)
+        s_q[...] = total.astype(BF16)
         for k in range(1, 4):
             to = ring(x, k)
-            c = copy(n, 5 + to, 5 + x, s_y.at[n, to], r_x.at[n, x], x_peer(k))
+            c = copy(n, 8 + to, 8 + x, s_q.at[:, to], r_x.at[x], x_peer(k))
             c.start()
             sends.append(c)
-        total = s_y[n, x].astype(F32)
+        total = s_q[:, x].astype(F32)
         for k in range(1, 4):
             at = ring(x, k)
-            copy(
-                n, 5 + at, 5 + at, s_y.at[n, at], r_x.at[n, at], x_peer(k)
-            ).wait_recv()
-            total = total + r_x[n, at].astype(F32)
+            copy(n, 8 + at, 8 + at, s_q.at[:, at], r_x.at[at], x_peer(k)).wait_recv()
+            total = total + r_x[at].astype(F32)
         return total
 
     def across(g):
-        return copy(2 * g, 9, 9, s_x.at[g, 1 - zh], r_z.at[g], zh_peer)
+        return copy(g, 12, 12, s_x.at[g, 1 - zh], r_z.at[g], zh_peer)
 
     def finish(g, out_ref):
         across(g).wait_recv()
@@ -226,21 +214,7 @@
         for a in range(NBL):
             out_ref[a] = total[2 * a : 2 * a + 2]
 
-    for s in others:
-        mg_copy(s, s).wait_recv()
-    for a in range(NBL):
-        cols = slice(a * BS, (a + 1) * BS)
-        pg = (recv_mg[a].astype(F32) * dgelu[a]).astype(BF16)
-        grad = dot_nn(pg, x_ref[:, cols]).astype(BF16)
-        part[a] = dot_tn(grad, placing).astype(BF16)
-        ig_ref[:, cols] = dot_tn(pg, wm[a]).astype(BF16)
-    for s in range(NBL):
-        g_core[s // 4, s % 4] = swapped(part, s).reshape(4, 2, 16, BS)
-    s_x[0, 0] = plane_sum(0)
-    s_x[0, 1] = plane_sum(1)
-    across(0).start()
-
-    def second(which, sources, h):
+    def second(sources, h, store):
         for s in sources:
             act_copy(s, s).wait_recv()
         rows = pl.ds(pl.multiple_of(h * 64, 64), 64)
@@ -248,16 +222,34 @@
             cols = slice(d * BS, (d + 1) * BS)
             part[d, :64] = dot_nn(recv_act[d, rows, :], og_ref[:, cols]).astype(BF16)
         for s in range(4):
-            g_core[which, s] = swapped(part, s).reshape(4, 2, 16, BS)
-        s_x[1, h] = plane_sum(which)
-
-    second(2, near, half)
+            store[s] = swapped(part, s).reshape(8, 16, BS)
+
+    for s in others:
+        mg_copy(s, s).wait_recv()
+    for a in range(NBL):
+        cols = slice(a * BS, (a + 1) * BS)
+        pg = (recv_mg[a].astype(F32) * dgelu[a]).astype(BF16)
+        tmp[a] = pg
+        grad = dot_nn(pg, x_ref[:, cols]).astype(BF16)
+        part[a] = dot_tn(grad, placing).astype(BF16)
+    for s in range(NBL):
+        g_early[s // 4, s % 4] = swapped(part, s).reshape(8, 16, BS)
+    second(near, half, g_early.at[2])
+    total = plane_sum(0, g_early, rq_early, sq_early, rx_early)
+    s_x[0] = total[:2]
+    s_x[1, half] = total[2]
+    across(0).start()
 
     @pl.when(zh != half)
     def _():
         across(1).start()
 
-    second(3, far, 1 - half)
+    for a in range(NBL):
+        cols = slice(a * BS, (a + 1) * BS)
+        ig_ref[:, cols] = dot_tn(tmp[a], wm[a]).astype(BF16)
+
+    second(far, 1 - half, g_late.at[0])
+    s_x[1, 1 - half] = plane_sum(1, g_late, rq_late, sq_late, rx_late)[0]
 
     @pl.when(zh == half)
     def _():
@@ -281,6 +273,7 @@
 def per_device(tokens, first_blocks, latter_factor_blocks, block_perm, out_grad):
     vmem = pl.BlockSpec(memory_space=pltpu.VMEM)
     hbm = pl.BlockSpec(memory_space=pltpu.HBM)
+    tokens, first_blocks, latter_factor_blocks, block_perm, out_grad = [pltpu.with_memory_space_constraint(v, pltpu.HBM) for v in (tokens, first_blocks, latter_factor_blocks, block_perm.reshape(1, 64), out_grad)]
     return pl.pallas_call(
         kernel,
         out_shape=(
@@ -305,25 +298,27 @@
             pltpu.VMEM((NBL, NBL, 16, ROWS), BF16),
             pltpu.VMEM((NBL, BS, ROWS), BF16),
             pltpu.VMEM((NBL, BS, BS), BF16),
-            pltpu.VMEM((4, 4, 4, 2, 16, BS), BF16),
-            pltpu.VMEM((4, 4, 4, 16, BS), BF16),
-            pltpu.VMEM((4, 4, 4, 16, BS), BF16),
-            pltpu.VMEM((4, 4, 4, 16, BS), BF16),
-            pltpu.VMEM((4, 4, 16, BS), BF16),
-            pltpu.VMEM((4, 4, 16, BS), BF16),
+            pltpu.VMEM((3, 4, 8, 16, BS), BF16),
+            pltpu.VMEM((8, 3, 4, 16, BS), BF16),
+            pltpu.VMEM((3, 4, 16, BS), BF16),
+            pltpu.VMEM((4, 3, 16, BS), BF16),
+            pltpu.VMEM((1, 4, 8, 16, BS), BF16),
+            pltpu.VMEM((8, 1, 4, 16, BS), BF16),
+            pltpu.VMEM((1, 4, 16, BS), BF16),
+            pltpu.VMEM((4, 1, 16, BS), BF16),
             pltpu.VMEM((2, 2, 16, BS), F32),
             pltpu.VMEM((2, 16, BS), F32),
             pltpu.SemaphoreType.DMA((2, NBL)),
             pltpu.SemaphoreType.DMA((2, NBL)),
-            pltpu.SemaphoreType.DMA((4, 10)),
-            pltpu.SemaphoreType.DMA((4, 10)),
+            pltpu.SemaphoreType.DMA((2, 13)),
+            pltpu.SemaphoreType.DMA((2, 13)),
             pltpu.SemaphoreType.REGULAR,
             pltpu.SemaphoreType.REGULAR,
         ],
         compiler_params=pltpu.CompilerParams(
-            collective_id=0, has_side_effects=True, vmem_limit_bytes=56 * 2**20
+            collective_id=0, has_side_effects=True, vmem_limit_bytes=24 * 2**20
         ),
-    )(tokens, first_blocks, latter_factor_blocks, block_perm.reshape(1, 64), out_grad)
+    )(tokens, first_blocks, latter_factor_blocks, block_perm, out_grad)
 
 
 def solution(mesh):

time: 94.3 us -> 77.1 us (0.82)
  Pallas kernels: 89.6 us -> 74.3 us
  local copies, waits for them, and re-layouts: 3.77 us -> 1.99 us
    pallas_call x1, Pallas kernels: 89.6 us -> 74.3 us  [per_device(): pl.pallas_call(kernel, out_shape=(jax.ShapeDtypeStruct((NBL, 2, BS), F32)...]
    unnamed x5 -> x3, local copies, waits for them, and re-layouts: 3.77 us -> 1.99 us
where the time goes in v3:
time: 77.1 us; the launch traced here: 77 us
  Pallas kernels  74.3 us (96%)
  local copies, waits for them, and re-layouts  1.99 us (3%)
    pallas_call x1, Pallas kernels, per_device(): pl.pallas_call(kernel, out_shape=(jax.ShapeDtypeStruct((NBL, 2, BS), F32)...  74.3 us
    unnamed x3, local copies, waits for them, and re-layouts  1.99 us

profile of v3, /device:TPU:128, one launch (start us, length us, event | category | flops | bytes accessed | tf_op | source)
XLA Modules:
  0.0 77.0 jit_solution(5761939197883405756)
XLA Ops:
  0.6 74.3 %shard_map.76 = (f32[8,2,128]{2,1,0:T(2,128)S(1)}, f32[8,2,128]{2,1,0:T(2,128)S(1)}, bf16[256,1024]{1,0:T(8,128)(2,1)S(1)}) custom-call(bf16[256,1024]{1,0:T(8,128)(2,1)} %x_hbm.1, bf16[8,128,128]{2,1,0:T(8,128)(2,1)} %w_hbm.1, bf16[8,128,128]{2,1,0:T(8,128)(2,1)} %l_hbm.1, s32[1,64]{1,0:T(1,128)} %bitcast.1, bf16[256,1024]{1,0:T(8,128)(2,1)} %og_hbm.1), custom_call_target="tpu_custom_call" | custom-call | tf_op jit(solution)/shard_map/pallas_call | solution.py:277
  75.0 0.6 copy.11
  75.6 0.6 copy.12
  76.2 0.8 %copy.13 = bf16[256,1024]{1,0:T(8,128)(2,1)} copy(bf16[256,1024]{1,0:T(8,128)(2,1)S(1)} %get-tuple-element.8) | data formatting | bytes 1048576

commit v4 on v3

--- a/solution.py
+++ b/solution.py
@@ -11,7 +11,6 @@
 ROWS = 256
 BS = 128
 NBL = 8
-HOLD = True
 
 
 def dot_nn(a, b):
@@ -38,9 +37,9 @@
     x_hbm, w_hbm, l_hbm, perm_hbm, og_hbm,
     fg_ref, lg_ref, ig_ref,
     x_ref, w_ref, l_ref, perm_ref, og_ref, in_sem,
-    wm, tmp, dgelu, send_mg, recv_mg, send_act, recv_act, part,
-    g_early, rq_early, sq_early, rx_early, g_late, rq_late, sq_late, rx_late, s_x, r_z,
-    a2a_send, a2a_recv, rs_send, rs_recv, edge_sem, open_sem,
+    wm, tmp, act, dgelu, send_mg, recv_mg, send_act, recv_act, part,
+    g_early, rq_early, sq_early, g_late, rq_late, sq_late, r_last,
+    a2a_send, a2a_recv, rs_send, rs_recv, last_send, last_recv, edge_sem, open_sem, open_x_sem, up_sem, down_sem,
 ):
     b = lax.axis_index("blk")
     t = lax.axis_index("tok")
@@ -69,10 +68,16 @@
         pl.semaphore_signal(sem, inc=1, device_id=peer, device_id_type=MESH)
 
     barrier = pltpu.get_barrier_semaphore()
-    peers = [(s, t) for s in others]
-    peers += [q_peer(k) for k in range(1, 8)] + [x_peer(k) for k in range(1, 4)]
-    for peer in peers:
+    for peer in [q_peer(k) for k in range(1, 8)] + [x_peer(k) for k in range(1, 4)]:
         signal(barrier, peer)
+
+    @pl.when(b > 0)
+    def _():
+        signal(barrier, (b - 1, t))
+
+    @pl.when(b < 7)
+    def _():
+        signal(barrier, (b + 1, t))
 
     @pl.when(at_edge)
     def _():
@@ -125,39 +130,72 @@
     for d in range(NBL):
         cols = slice(d * BS, (d + 1) * BS)
         tmp[d] = dot_nt(l_ref[d], og_ref[:, cols]).astype(BF16)
-    for at, s in enumerate(others):
-        send_mg[s] = swapped(tmp, s)
-        if at == 0:
-            pl.semaphore_wait(barrier, len(peers) + jnp.where(at_edge, 1, 0))
-        mg_copy(s, b).start()
-    recv_mg[:, slab(b), :] = swapped(tmp, b)
-
-    @pl.when(at_edge)
-    def _():
-        signal(edge_sem, edge_peer)
-
+
+    def entered(k):
+        up, down = b + k, b - k
+
+        @pl.when(down >= 0)
+        def _():
+            if k > 1:
+                pl.semaphore_wait(down_sem.at[k], 1)
+            if k < 7:
+
+                @pl.when(b < 7)
+                def _():
+                    signal(down_sem.at[k + 1], (b + 1, t))
+
+            send_mg[down] = swapped(tmp, down)
+            mg_copy(down, b).start()
+
+        @pl.when(up < 8)
+        def _():
+            if k > 1:
+                pl.semaphore_wait(up_sem.at[k], 1)
+            if k < 7:
+
+                @pl.when(b > 0)
+                def _():
+                    signal(up_sem.at[k + 1], (b - 1, t))
+
+            send_mg[up] = swapped(tmp, up)
+            mg_copy(up, b).start()
+
+    def activation(a):
+        cols = slice(a * BS, (a + 1) * BS)
+        wm[a] = dot_nt(placing, w_ref[a]).astype(BF16)
+        pre = dot_nt(wm[a], x_ref[:, cols])
+        cdf = 0.5 * (1.0 + lax.erf(pre * 0.7071067811865476))
+        act[a] = (pre * cdf).astype(BF16)
+        dgelu[a] = cdf + pre * 0.3989422804014327 * jnp.exp(-0.5 * pre * pre)
+
+    pl.semaphore_wait(
+        barrier, 10 + jnp.where(b > 0, 1, 0) + jnp.where(b < 7, 1, 0) + jnp.where(at_edge, 1, 0)
+    )
+    entered(1)
     for load in loads[2:]:
         load.wait()
     perm = jnp.broadcast_to(perm_ref[...].astype(F32), (16, 64)).astype(BF16)
     pair = one_hot(iota(1)[:64] // 2 == iota(0)[:64])
     target = dot_nn(perm, pair)[:1] * 2.0 + (iota(1)[:1] % 2).astype(F32)
     placing = one_hot(iota(0).astype(F32) == target)
-    for a in range(NBL):
-        cols = slice(a * BS, (a + 1) * BS)
-        wm[a] = dot_nt(placing, w_ref[a]).astype(BF16)
-        pre = dot_nt(wm[a], x_ref[:, cols])
-        cdf = 0.5 * (1.0 + lax.erf(pre * 0.7071067811865476))
-        tmp[a] = (pre * cdf).astype(BF16)
-        dgelu[a] = cdf + pre * 0.3989422804014327 * jnp.exp(-0.5 * pre * pre)
-    for s in near + far:
-        send_act[s] = swapped(tmp, s)
-    recv_act[:, slab(b), :] = swapped(tmp, b)
+    for k in range(2, 6):
+        activation(2 * k - 4)
+        activation(2 * k - 3)
+        entered(k)
+    entered(6)
+    entered(7)
+    recv_mg[:, slab(b), :] = swapped(tmp, b)
+
+    @pl.when(at_edge)
+    def _():
+        signal(edge_sem, edge_peer)
+
     for s in near:
+        send_act[s] = swapped(act, s)
         act_copy(s, b).start()
     for s in far:
-        if HOLD:
-            mg_copy(s, b).wait_send()
-        act_copy(s, b).start()
+        send_act[s] = swapped(act, s)
+    recv_act[:, slab(b), :] = swapped(act, b)
 
     @pl.when(at_edge)
     def _():
@@ -169,48 +207,86 @@
     def _():
         pl.semaphore_wait(open_sem, 1)
 
+    for k in range(1, 4):
+        signal(open_x_sem, x_peer(k))
+
+    for s in others:
+        mg_copy(s, s).wait_recv()
+    for s in far:
+        act_copy(s, b).start()
+
     sends = []
 
-    def copy(n, at_src, at_dst, src, dst, peer):
+    def copy(send_sem, recv_sem, n, at_src, at_dst, src, dst, peer):
         return pltpu.make_async_remote_copy(
             src_ref=src,
             dst_ref=dst,
-            send_sem=rs_send.at[n, at_src],
-            recv_sem=rs_recv.at[n, at_dst],
+            send_sem=send_sem.at[n, at_src],
+            recv_sem=recv_sem.at[n, at_dst],
             device_id=peer,
             device_id_type=MESH,
         )
 
-    def plane_sum(n, g, r_q, s_q, r_x):
+    def q_sum(n, g, r_q, s_q):
         for k in range(1, 8):
             to = (q + k) % 8
-            c = copy(n, to, q, g.at[:, :, to], r_q.at[q], q_peer(k))
+            c = copy(rs_send, rs_recv, n, to, q, g.at[:, :, to], r_q.at[q], q_peer(k))
             c.start()
             sends.append(c)
         total = g[:, :, q].astype(F32)
         for k in range(1, 8):
             at = (q + k) % 8
-            copy(n, at, at, g.at[:, :, at], r_q.at[at], q_peer(k)).wait_recv()
+            copy(
+                rs_send, rs_recv, n, at, at, g.at[:, :, at], r_q.at[at], q_peer(k)
+            ).wait_recv()
             total = total + r_q[at].astype(F32)
         s_q[...] = total.astype(BF16)
+
+    def last_copy(u, g, h, k, src):
+        to = ring(x, k)
+        return pltpu.make_async_remote_copy(
+            src_ref=src.at[to],
+            dst_ref=r_last.at[g, zh * 4 + x],
+            send_sem=last_send.at[u, to],
+            recv_sem=last_recv.at[g, zh * 4 + x],
+            device_id=(b, h * 32 + to * 8 + q),
+            device_id_type=MESH,
+        )
+
+    def last_start(*which):
         for k in range(1, 4):
-            to = ring(x, k)
-            c = copy(n, 8 + to, 8 + x, s_q.at[:, to], r_x.at[x], x_peer(k))
-            c.start()
-            sends.append(c)
-        total = s_q[:, x].astype(F32)
+            last_copy(*which[:3], k, which[3]).start()
+
+        @pl.when(zh != which[2])
+        def _():
+            last_copy(*which[:3], 0, which[3]).start()
+
+        @pl.when(zh == which[2])
+        def _():
+            r_last[which[1], zh * 4 + x] = which[3][x]
+
+    def last_drain(*which):
         for k in range(1, 4):
-            at = ring(x, k)
-            copy(n, 8 + at, 8 + at, s_q.at[:, at], r_x.at[at], x_peer(k)).wait_recv()
-            total = total + r_x[at].astype(F32)
-        return total
-
-    def across(g):
-        return copy(g, 12, 12, s_x.at[g, 1 - zh], r_z.at[g], zh_peer)
+            last_copy(*which[:3], k, which[3]).wait_send()
+
+        @pl.when(zh != which[2])
+        def _():
+            last_copy(*which[:3], 0, which[3]).wait_send()
 
     def finish(g, out_ref):
-        across(g).wait_recv()
-        total = s_x[g, zh] + r_z[g]
+        for k in range(1, 8):
+            at = (zh * 4 + x + k) % 8
+            pltpu.make_async_remote_copy(
+                src_ref=r_last.at[g, at],
+                dst_ref=r_last.at[g, at],
+                send_sem=last_send.at[g, 0],
+                recv_sem=last_recv.at[g, at],
+                device_id=zh_peer,
+                device_id_type=MESH,
+            ).wait_recv()
+        total = r_last[g, 0].astype(F32)
+        for at in range(1, 8):
+            total = total + r_last[g, at].astype(F32)
         for a in range(NBL):
             out_ref[a] = total[2 * a : 2 * a + 2]
 
@@ -224,8 +300,6 @@
         for s in range(4):
             store[s] = swapped(part, s).reshape(8, 16, BS)
 
-    for s in others:
-        mg_copy(s, s).wait_recv()
     for a in range(NBL):
         cols = slice(a * BS, (a + 1) * BS)
         pg = (recv_mg[a].astype(F32) * dgelu[a]).astype(BF16)
@@ -235,39 +309,34 @@
     for s in range(NBL):
         g_early[s // 4, s % 4] = swapped(part, s).reshape(8, 16, BS)
     second(near, half, g_early.at[2])
-    total = plane_sum(0, g_early, rq_early, sq_early, rx_early)
-    s_x[0] = total[:2]
-    s_x[1, half] = total[2]
-    across(0).start()
-
-    @pl.when(zh != half)
-    def _():
-        across(1).start()
+    q_sum(0, g_early, rq_early, sq_early)
+    pl.semaphore_wait(open_x_sem, 3)
+    lasts = [
+        (0, 0, 0, sq_early.at[0]),
+        (1, 0, 1, sq_early.at[1]),
+        (2, 1, half, sq_early.at[2]),
+        (3, 1, 1 - half, sq_late.at[0]),
+    ]
+    for last in lasts[:3]:
+        last_start(*last)
 
     for a in range(NBL):
         cols = slice(a * BS, (a + 1) * BS)
         ig_ref[:, cols] = dot_tn(tmp[a], wm[a]).astype(BF16)
 
     second(far, 1 - half, g_late.at[0])
-    s_x[1, 1 - half] = plane_sum(1, g_late, rq_late, sq_late, rx_late)[0]
-
-    @pl.when(zh == half)
-    def _():
-        across(1).start()
+    q_sum(1, g_late, rq_late, sq_late)
+    last_start(*lasts[3])
 
     finish(0, fg_ref)
     finish(1, lg_ref)
     for s in others:
-        if not HOLD:
-            mg_copy(s, b).wait_send()
+        mg_copy(s, b).wait_send()
         act_copy(s, b).wait_send()
-    if HOLD:
-        for s in near:
-            mg_copy(s, b).wait_send()
     for c in sends:
         c.wait_send()
-    across(0).wait_send()
-    across(1).wait_send()
+    for last in lasts:
+        last_drain(*last)
 
 
 def per_device(tokens, first_blocks, latter_factor_blocks, block_perm, out_grad):
@@ -292,6 +361,7 @@
             pltpu.SemaphoreType.DMA((5,)),
             pltpu.VMEM((NBL, BS, BS), BF16),
             pltpu.VMEM((NBL, BS, ROWS), BF16),
+            pltpu.VMEM((NBL, BS, ROWS), BF16),
             pltpu.VMEM((NBL, BS, ROWS), F32),
             pltpu.VMEM((NBL, NBL, 16, ROWS), BF16),
             pltpu.VMEM((NBL, BS, ROWS), BF16),
@@ -301,19 +371,21 @@
             pltpu.VMEM((3, 4, 8, 16, BS), BF16),
             pltpu.VMEM((8, 3, 4, 16, BS), BF16),
             pltpu.VMEM((3, 4, 16, BS), BF16),
-            pltpu.VMEM((4, 3, 16, BS), BF16),
             pltpu.VMEM((1, 4, 8, 16, BS), BF16),
             pltpu.VMEM((8, 1, 4, 16, BS), BF16),
             pltpu.VMEM((1, 4, 16, BS), BF16),
-            pltpu.VMEM((4, 1, 16, BS), BF16),
-            pltpu.VMEM((2, 2, 16, BS), F32),
-            pltpu.VMEM((2, 16, BS), F32),
+            pltpu.VMEM((2, 8, 16, BS), BF16),
             pltpu.SemaphoreType.DMA((2, NBL)),
             pltpu.SemaphoreType.DMA((2, NBL)),
-            pltpu.SemaphoreType.DMA((2, 13)),
-            pltpu.SemaphoreType.DMA((2, 13)),
+            pltpu.SemaphoreType.DMA((2, 8)),
+            pltpu.SemaphoreType.DMA((2, 8)),
+            pltpu.SemaphoreType.DMA((4, 4)),
+            pltpu.SemaphoreType.DMA((2, 8)),
             pltpu.SemaphoreType.REGULAR,
             pltpu.SemaphoreType.REGULAR,
+            pltpu.SemaphoreType.REGULAR,
+            pltpu.SemaphoreType.REGULAR((8,)),
+            pltpu.SemaphoreType.REGULAR((8,)),
         ],
         compiler_params=pltpu.CompilerParams(
             collective_id=0, has_side_effects=True, vmem_limit_bytes=24 * 2**20

time: 77.1 us -> 75.8 us (0.983)
  the two profiles are of different devices: /device:TPU:128 before, /device:TPU:192 now
where the time goes in v4:
time: 75.8 us; the launch traced here: 75.6 us
  Pallas kernels  73 us (96%)
  local copies, waits for them, and re-layouts  1.99 us (3%)
    pallas_call x1, Pallas kernels, per_device(): pl.pallas_call(kernel, out_shape=(jax.ShapeDtypeStruct((NBL, 2, BS), F32)...  73 us
    unnamed x3, local copies, waits for them, and re-layouts  1.99 us

profile of v4, /device:TPU:192, one launch (start us, length us, event | category | flops | bytes accessed | tf_op | source)
XLA Modules:
  0.0 75.6 jit_solution(2094332156291255501)
XLA Ops:
  0.6 73.0 %shard_map.76 = (f32[8,2,128]{2,1,0:T(2,128)S(1)}, f32[8,2,128]{2,1,0:T(2,128)S(1)}, bf16[256,1024]{1,0:T(8,128)(2,1)S(1)}) custom-call(bf16[256,1024]{1,0:T(8,128)(2,1)} %x_hbm.1, bf16[8,128,128]{2,1,0:T(8,128)(2,1)} %w_hbm.1, bf16[8,128,128]{2,1,0:T(8,128)(2,1)} %l_hbm.1, s32[1,64]{1,0:T(1,128)} %bitcast.1, bf16[256,1024]{1,0:T(8,128)(2,1)} %og_hbm.1), custom_call_target="tpu_custom_call" | custom-call | tf_op jit(solution)/shard_map/pallas_call | solution.py:346
  73.6 0.6 copy.11
  74.2 0.6 copy.12
  74.8 0.8 %copy.13 = bf16[256,1024]{1,0:T(8,128)(2,1)} copy(bf16[256,1024]{1,0:T(8,128)(2,1)S(1)} %get-tuple-element.8) | data formatting | bytes 1048576

commit v5 on v4

--- a/solution.py
+++ b/solution.py
@@ -39,7 +39,7 @@
     x_ref, w_ref, l_ref, perm_ref, og_ref, in_sem,
     wm, tmp, act, dgelu, send_mg, recv_mg, send_act, recv_act, part,
     g_early, rq_early, sq_early, g_late, rq_late, sq_late, r_last,
-    a2a_send, a2a_recv, rs_send, rs_recv, last_send, last_recv, edge_sem, open_sem, open_x_sem, up_sem, down_sem,
+    a2a_send, a2a_recv, rs_send, rs_recv, last_send, last_recv, edge_sem, edge_x_sem, open_sem, up_sem, down_sem,
 ):
     b = lax.axis_index("blk")
     t = lax.axis_index("tok")
@@ -57,7 +57,7 @@
     def x_peer(k):
         return (b, t + (ring(x, k) - x) * 8)
 
-    far = [(1 - half) * 4 + ring(place, k) for k in range(4)]
+    far = [half * (3 - k) + (1 - half) * (4 + k) for k in range(4)]
     near = [half * 4 + ring(place, k) for k in range(1, 4)]
     others = far + near
 
@@ -68,8 +68,7 @@
         pl.semaphore_signal(sem, inc=1, device_id=peer, device_id_type=MESH)
 
     barrier = pltpu.get_barrier_semaphore()
-    for peer in [q_peer(k) for k in range(1, 8)] + [x_peer(k) for k in range(1, 4)]:
-        signal(barrier, peer)
+    plane = [q_peer(k) for k in range(1, 8)] + [x_peer(k) for k in range(1, 4)]
 
     @pl.when(b > 0)
     def _():
@@ -81,7 +80,8 @@
 
     @pl.when(at_edge)
     def _():
-        signal(barrier, edge_peer)
+        for peer in [*plane, edge_peer]:
+            signal(barrier, peer)
 
     loads = [
         pltpu.make_async_copy(src, dst, in_sem.at[i])
@@ -169,7 +169,8 @@
         dgelu[a] = cdf + pre * 0.3989422804014327 * jnp.exp(-0.5 * pre * pre)
 
     pl.semaphore_wait(
-        barrier, 10 + jnp.where(b > 0, 1, 0) + jnp.where(b < 7, 1, 0) + jnp.where(at_edge, 1, 0)
+        barrier,
+        jnp.where(b > 0, 1, 0) + jnp.where(b < 7, 1, 0) + jnp.where(at_edge, 11, 0),
     )
     entered(1)
     for load in loads[2:]:
@@ -188,7 +189,8 @@
 
     @pl.when(at_edge)
     def _():
-        signal(edge_sem, edge_peer)
+        for peer in [*plane, edge_peer]:
+            signal(edge_sem, peer)
 
     for s in near:
         send_act[s] = swapped(act, s)
@@ -197,9 +199,15 @@
         send_act[s] = swapped(act, s)
     recv_act[:, slab(b), :] = swapped(act, b)
 
+    for s in far:
+        act_copy(s, b).start()
+
     @pl.when(at_edge)
     def _():
-        pl.semaphore_wait(edge_sem, 1)
+        pl.semaphore_wait(edge_sem, 11)
+        for k in range(1, 4):
+            signal(edge_x_sem, x_peer(k))
+        pl.semaphore_wait(edge_x_sem, 3)
         for k in range(1, 8):
             signal(open_sem, ((b + k) % 8, t))
 
@@ -207,13 +215,8 @@
     def _():
         pl.semaphore_wait(open_sem, 1)
 
-    for k in range(1, 4):
-        signal(open_x_sem, x_peer(k))
-
     for s in others:
         mg_copy(s, s).wait_recv()
-    for s in far:
-        act_copy(s, b).start()
 
     sends = []
 
@@ -310,7 +313,6 @@
         g_early[s // 4, s % 4] = swapped(part, s).reshape(8, 16, BS)
     second(near, half, g_early.at[2])
     q_sum(0, g_early, rq_early, sq_early)
-    pl.semaphore_wait(open_x_sem, 3)
     lasts = [
         (0, 0, 0, sq_early.at[0]),
         (1, 0, 1, sq_early.at[1]),
@@ -339,11 +341,22 @@
         last_drain(*last)
 
 
+def publish(fg_in, lg_in, ig_in, fg_out, lg_out, ig_out, sem):
+    copies = [
+        pltpu.make_async_copy(src, dst, sem.at[i])
+        for i, (src, dst) in enumerate(((ig_in, ig_out), (fg_in, fg_out), (lg_in, lg_out)))
+    ]
+    for copy in copies:
+        copy.start()
+    for copy in copies:
+        copy.wait()
+
+
 def per_device(tokens, first_blocks, latter_factor_blocks, block_perm, out_grad):
     vmem = pl.BlockSpec(memory_space=pltpu.VMEM)
     hbm = pl.BlockSpec(memory_space=pltpu.HBM)
     tokens, first_blocks, latter_factor_blocks, block_perm, out_grad = [pltpu.with_memory_space_constraint(v, pltpu.HBM) for v in (tokens, first_blocks, latter_factor_blocks, block_perm.reshape(1, 64), out_grad)]
-    return pl.pallas_call(
+    outs = pl.pallas_call(
         kernel,
         out_shape=(
             jax.ShapeDtypeStruct((NBL, 2, BS), F32),
@@ -391,6 +404,14 @@
             collective_id=0, has_side_effects=True, vmem_limit_bytes=24 * 2**20
         ),
     )(tokens, first_blocks, latter_factor_blocks, block_perm, out_grad)
+    return pl.pallas_call(
+        publish,
+        out_shape=tuple(jax.ShapeDtypeStruct(o.shape, o.dtype) for o in outs),
+        in_specs=[vmem] * 3,
+        out_specs=[hbm] * 3,
+        scratch_shapes=[pltpu.SemaphoreType.DMA((3,))],
+        compiler_params=pltpu.CompilerParams(vmem_limit_bytes=16 * 2**20),
+    )(*outs)
 
 
 def solution(mesh):

time: 75.8 us -> 73.1 us (0.964)
  the two profiles are of different devices: /device:TPU:192 before, /device:TPU:224 now
where the time goes in v5:
time: 73.1 us; the launch traced here: 73 us
  Pallas kernels  72.3 us (99%)
    pallas_call x1, Pallas kernels, per_device(): pl.pallas_call(kernel, out_shape=(jax.ShapeDtypeStruct((NBL, 2, BS), F32)...  71.5 us

profile of v5, /device:TPU:224, one launch (start us, length us, event | category | flops | bytes accessed | tf_op | source)
XLA Modules:
  0.0 73.0 jit_solution(17307414182613195924)
XLA Ops:
  0.6 71.5 %shard_map.76 = (f32[8,2,128]{2,1,0:T(2,128)S(1)}, f32[8,2,128]{2,1,0:T(2,128)S(1)}, bf16[256,1024]{1,0:T(8,128)(2,1)S(1)}) custom-call(bf16[256,1024]{1,0:T(8,128)(2,1)} %x_hbm.1, bf16[8,128,128]{2,1,0:T(8,128)(2,1)} %w_hbm.1, bf16[8,128,128]{2,1,0:T(8,128)(2,1)} %l_hbm.1, s32[1,64]{1,0:T(1,128)} %bitcast.1, bf16[256,1024]{1,0:T(8,128)(2,1)} %og_hbm.1), custom_call_target="tpu_custom_call" | custom-call | tf_op jit(solution)/shard_map/pallas_call | solution.py:359
  72.1 0.8 %shard_map.77 = (f32[8,2,128]{2,1,0:T(2,128)}, f32[8,2,128]{2,1,0:T(2,128)}, bf16[256,1024]{1,0:T(8,128)(2,1)}) custom-call(f32[8,2,128]{2,1,0:T(2,128)S(1)} %get-tuple-element.6.fg_in, f32[8,2,128]{2,1,0:T(2,128)S(1)} %get-tuple-element.7.lg_in, bf16[256,1024]{1,0:T(8,128)(2,1)S(1)} %get-tuple-element.8.ig_in), custom_call_target="tpu_custom_call" | custom-call | tf_op jit(solution)/shard_map/pallas_call | solution.py:407

commit v6 on v5

--- a/solution.py
+++ b/solution.py
@@ -38,8 +38,8 @@
     fg_ref, lg_ref, ig_ref,
     x_ref, w_ref, l_ref, perm_ref, og_ref, in_sem,
     wm, tmp, act, dgelu, send_mg, recv_mg, send_act, recv_act, part,
-    g_early, rq_early, sq_early, g_late, rq_late, sq_late, r_last,
-    a2a_send, a2a_recv, rs_send, rs_recv, last_send, last_recv, edge_sem, edge_x_sem, open_sem, up_sem, down_sem,
+    g_early, rq_early, sq_early, g_late, rq_late, sq_late, r_last, r_x, s_x, r_across,
+    a2a_send, a2a_recv, rs_send, rs_recv, last_send, last_recv, x_send, x_recv, across_send, across_recv, edge_sem, edge_x_sem, open_sem, up_sem, down_sem,
 ):
     b = lax.axis_index("blk")
     t = lax.axis_index("tok")
@@ -60,6 +60,7 @@
     far = [half * (3 - k) + (1 - half) * (4 + k) for k in range(4)]
     near = [half * 4 + ring(place, k) for k in range(1, 4)]
     others = far + near
+    inner = half * place + (1 - half) * (3 - place)
 
     at_edge = b == 7 - 7 * zh
     edge_peer = (7 - b, t + 32 - 64 * zh)
@@ -199,8 +200,10 @@
         send_act[s] = swapped(act, s)
     recv_act[:, slab(b), :] = swapped(act, b)
 
-    for s in far:
-        act_copy(s, b).start()
+    @pl.when(jnp.logical_not(inner >= 3))
+    def _():
+        for s in far:
+            act_copy(s, b).start()
 
     @pl.when(at_edge)
     def _():
@@ -217,6 +220,11 @@
 
     for s in others:
         mg_copy(s, s).wait_recv()
+
+    @pl.when(inner >= 3)
+    def _():
+        for s in far:
+            act_copy(s, b).start()
 
     sends = []
 
@@ -276,20 +284,27 @@
         def _():
             last_copy(*which[:3], 0, which[3]).wait_send()
 
-    def finish(g, out_ref):
-        for k in range(1, 8):
-            at = (zh * 4 + x + k) % 8
-            pltpu.make_async_remote_copy(
-                src_ref=r_last.at[g, at],
-                dst_ref=r_last.at[g, at],
-                send_sem=last_send.at[g, 0],
-                recv_sem=last_recv.at[g, at],
-                device_id=zh_peer,
-                device_id_type=MESH,
-            ).wait_recv()
-        total = r_last[g, 0].astype(F32)
-        for at in range(1, 8):
-            total = total + r_last[g, at].astype(F32)
+    def across(g, src):
+        return pltpu.make_async_remote_copy(
+            src_ref=src,
+            dst_ref=r_across.at[g],
+            send_sem=across_send.at[g],
+            recv_sem=across_recv.at[g],
+            device_id=zh_peer,
+            device_id_type=MESH,
+        )
+
+    def early_copy(to, at, k):
+        return pltpu.make_async_remote_copy(
+            src_ref=sq_early.at[:, to],
+            dst_ref=r_x.at[at],
+            send_sem=x_send.at[to],
+            recv_sem=x_recv.at[at],
+            device_id=x_peer(k),
+            device_id_type=MESH,
+        )
+
+    def put(total, out_ref):
         for a in range(NBL):
             out_ref[a] = total[2 * a : 2 * a + 2]
 
@@ -313,14 +328,19 @@
         g_early[s // 4, s % 4] = swapped(part, s).reshape(8, 16, BS)
     second(near, half, g_early.at[2])
     q_sum(0, g_early, rq_early, sq_early)
-    lasts = [
-        (0, 0, 0, sq_early.at[0]),
-        (1, 0, 1, sq_early.at[1]),
-        (2, 1, half, sq_early.at[2]),
-        (3, 1, 1 - half, sq_late.at[0]),
-    ]
-    for last in lasts[:3]:
-        last_start(*last)
+    for k in range(1, 4):
+        early_copy(ring(x, k), x, k).start()
+    total = sq_early[:, x].astype(F32)
+    for k in range(1, 4):
+        at = ring(x, k)
+        early_copy(at, at, k).wait_recv()
+        total = total + r_x[at].astype(F32)
+    s_x[...] = total.astype(BF16)
+    across(0, s_x.at[1 - zh]).start()
+
+    @pl.when(zh != half)
+    def _():
+        across(1, s_x.at[2]).start()
 
     for a in range(NBL):
         cols = slice(a * BS, (a + 1) * BS)
@@ -328,17 +348,47 @@
 
     second(far, 1 - half, g_late.at[0])
     q_sum(1, g_late, rq_late, sq_late)
-    last_start(*lasts[3])
-
-    finish(0, fg_ref)
-    finish(1, lg_ref)
+    last = (0, 0, 1 - half, sq_late.at[0])
+    last_start(*last)
+
+    across(0, s_x.at[1 - zh]).wait_recv()
+    put(s_x[zh].astype(F32) + r_across[0].astype(F32), fg_ref)
+
+    @pl.when(zh == half)
+    def _():
+        across(1, s_x.at[2]).wait_recv()
+        put(s_x[2].astype(F32) + r_across[1].astype(F32), lg_ref)
+
+    @pl.when(zh != half)
+    def _():
+        for k in range(1, 8):
+            at = (zh * 4 + x + k) % 8
+            pltpu.make_async_remote_copy(
+                src_ref=r_last.at[0, at],
+                dst_ref=r_last.at[0, at],
+                send_sem=last_send.at[0, 0],
+                recv_sem=last_recv.at[0, at],
+                device_id=zh_peer,
+                device_id_type=MESH,
+            ).wait_recv()
+        total = r_last[0, 0].astype(F32)
+        for at in range(1, 8):
+            total = total + r_last[0, at].astype(F32)
+        put(total, lg_ref)
+
     for s in others:
         mg_copy(s, b).wait_send()
         act_copy(s, b).wait_send()
     for c in sends:
         c.wait_send()
-    for last in lasts:
-        last_drain(*last)
+    last_drain(*last)
+    for k in range(1, 4):
+        early_copy(ring(x, k), x, k).wait_send()
+    across(0, s_x.at[1 - zh]).wait_send()
+
+    @pl.when(zh != half)
+    def _():
+        across(1, s_x.at[2]).wait_send()
 
 
 def publish(fg_in, lg_in, ig_in, fg_out, lg_out, ig_out, sem):
@@ -387,13 +437,20 @@
             pltpu.VMEM((1, 4, 8, 16, BS), BF16),
             pltpu.VMEM((8, 1, 4, 16, BS), BF16),
             pltpu.VMEM((1, 4, 16, BS), BF16),
-            pltpu.VMEM((2, 8, 16, BS), BF16),
+            pltpu.VMEM((1, 8, 16, BS), BF16),
+            pltpu.VMEM((4, 3, 16, BS), BF16),
+            pltpu.VMEM((3, 16, BS), BF16),
+            pltpu.VMEM((2, 16, BS), BF16),
             pltpu.SemaphoreType.DMA((2, NBL)),
             pltpu.SemaphoreType.DMA((2, NBL)),
             pltpu.SemaphoreType.DMA((2, 8)),
             pltpu.SemaphoreType.DMA((2, 8)),
-            pltpu.SemaphoreType.DMA((4, 4)),
-            pltpu.SemaphoreType.DMA((2, 8)),
+            pltpu.SemaphoreType.DMA((1, 4)),
+            pltpu.SemaphoreType.DMA((1, 8)),
+            pltpu.SemaphoreType.DMA((4,)),
+            pltpu.SemaphoreType.DMA((4,)),
+            pltpu.SemaphoreType.DMA((2,)),
+            pltpu.SemaphoreType.DMA((2,)),
             pltpu.SemaphoreType.REGULAR,
             pltpu.SemaphoreType.REGULAR,
             pltpu.SemaphoreType.REGULAR,

time: 73.1 us -> 71.1 us (0.973)
  Pallas kernels: 72.3 us -> 70.3 us
    pallas_call x1, Pallas kernels: 71.5 us -> 69.5 us  [per_device(): pl.pallas_call(kernel, out_shape=(jax.ShapeDtypeStruct((NBL, 2, BS), F32)...]
where the time goes in v6:
time: 71.1 us; the launch traced here: 71 us
  Pallas kernels  70.3 us (99%)
    pallas_call x1, Pallas kernels, per_device(): pl.pallas_call(kernel, out_shape=(jax.ShapeDtypeStruct((NBL, 2, BS), F32)...  69.5 us

profile of v6, /device:TPU:224, one launch (start us, length us, event | category | flops | bytes accessed | tf_op | source)
XLA Modules:
  0.0 71.0 jit_solution(15295059105155808429)
XLA Ops:
  0.6 69.5 %shard_map.76 = (f32[8,2,128]{2,1,0:T(2,128)S(1)}, f32[8,2,128]{2,1,0:T(2,128)S(1)}, bf16[256,1024]{1,0:T(8,128)(2,1)S(1)}) custom-call(bf16[256,1024]{1,0:T(8,128)(2,1)} %x_hbm.1, bf16[8,128,128]{2,1,0:T(8,128)(2,1)} %w_hbm.1, bf16[8,128,128]{2,1,0:T(8,128)(2,1)} %l_hbm.1, s32[1,64]{1,0:T(1,128)} %bitcast.1, bf16[256,1024]{1,0:T(8,128)(2,1)} %og_hbm.1), custom_call_target="tpu_custom_call" | custom-call | tf_op jit(solution)/shard_map/pallas_call | solution.py:409
  70.2 0.8 %shard_map.77 = (f32[8,2,128]{2,1,0:T(2,128)}, f32[8,2,128]{2,1,0:T(2,128)}, bf16[256,1024]{1,0:T(8,128)(2,1)}) custom-call(f32[8,2,128]{2,1,0:T(2,128)S(1)} %get-tuple-element.6.fg_in, f32[8,2,128]{2,1,0:T(2,128)S(1)} %get-tuple-element.7.lg_in, bf16[256,1024]{1,0:T(8,128)(2,1)S(1)} %get-tuple-element.8.ig_in), custom_call_target="tpu_custom_call" | custom-call | tf_op jit(solution)/shard_map/pallas_call | solution.py:464

commit v7 on v6

--- a/solution.py
+++ b/solution.py
@@ -238,20 +238,18 @@
             device_id_type=MESH,
         )
 
-    def q_sum(n, g, r_q, s_q):
+    def q_sum(n, src, land):
         for k in range(1, 8):
             to = (q + k) % 8
-            c = copy(rs_send, rs_recv, n, to, q, g.at[:, :, to], r_q.at[q], q_peer(k))
+            c = copy(rs_send, rs_recv, n, to, q, src(to), land(q), q_peer(k))
             c.start()
             sends.append(c)
-        total = g[:, :, q].astype(F32)
+        total = src(q)[...].astype(F32)
         for k in range(1, 8):
             at = (q + k) % 8
-            copy(
-                rs_send, rs_recv, n, at, at, g.at[:, :, at], r_q.at[at], q_peer(k)
-            ).wait_recv()
-            total = total + r_q[at].astype(F32)
-        s_q[...] = total.astype(BF16)
+            copy(rs_send, rs_recv, n, at, at, src(at), land(at), q_peer(k)).wait_recv()
+            total = total + land(at)[...].astype(F32)
+        return total.astype(BF16)
 
     def last_copy(u, g, h, k, src):
         to = ring(x, k)
@@ -264,17 +262,19 @@
             device_id_type=MESH,
         )
 
-    def last_start(*which):
-        for k in range(1, 4):
-            last_copy(*which[:3], k, which[3]).start()
-
-        @pl.when(zh != which[2])
+    def last_start(h, pick):
+        for k in range(4):
+            goes = pick(ring(x, k))
+            if k == 0:
+                goes = jnp.logical_and(goes, zh != h)
+
+            @pl.when(goes)
+            def _():
+                last_copy(0, 0, h, k, sq_late.at[0]).start()
+
+        @pl.when(jnp.logical_and(pick(x), zh == h))
         def _():
-            last_copy(*which[:3], 0, which[3]).start()
-
-        @pl.when(zh == which[2])
-        def _():
-            r_last[which[1], zh * 4 + x] = which[3][x]
+            r_last[0, zh * 4 + x] = sq_late[0, x]
 
     def last_drain(*which):
         for k in range(1, 4):
@@ -308,15 +308,17 @@
         for a in range(NBL):
             out_ref[a] = total[2 * a : 2 * a + 2]
 
-    def second(sources, h, store):
+    def second(at, count, sources, store):
         for s in sources:
             act_copy(s, s).wait_recv()
-        rows = pl.ds(pl.multiple_of(h * 64, 64), 64)
+        rows = pl.ds(pl.multiple_of(at * 16, 16), count * 16)
         for d in range(NBL):
             cols = slice(d * BS, (d + 1) * BS)
-            part[d, :64] = dot_nn(recv_act[d, rows, :], og_ref[:, cols]).astype(BF16)
-        for s in range(4):
-            store[s] = swapped(part, s).reshape(8, 16, BS)
+            part[d, : count * 16] = dot_nn(
+                recv_act[d, rows, :], og_ref[:, cols]
+            ).astype(BF16)
+        for s in range(count):
+            store[at % 4 + s] = swapped(part, s).reshape(8, 16, BS)
 
     for a in range(NBL):
         cols = slice(a * BS, (a + 1) * BS)
@@ -326,8 +328,8 @@
         part[a] = dot_tn(grad, placing).astype(BF16)
     for s in range(NBL):
         g_early[s // 4, s % 4] = swapped(part, s).reshape(8, 16, BS)
-    second(near, half, g_early.at[2])
-    q_sum(0, g_early, rq_early, sq_early)
+    second(4 * half, 4, near, g_early.at[2])
+    sq_early[...] = q_sum(0, lambda to: g_early.at[:, :, to], lambda at: rq_early.at[at])
     for k in range(1, 4):
         early_copy(ring(x, k), x, k).start()
     total = sq_early[:, x].astype(F32)
@@ -346,10 +348,19 @@
         cols = slice(a * BS, (a + 1) * BS)
         ig_ref[:, cols] = dot_tn(tmp[a], wm[a]).astype(BF16)
 
-    second(far, 1 - half, g_late.at[0])
-    q_sum(1, g_late, rq_late, sq_late)
+    inmost = 3 * half
+    outer = pl.ds(1 - half, 3)
+    second(4 - 4 * half + 1 - half, 3, far[1:], g_late.at[0])
+    sq_late[0, outer] = q_sum(
+        1, lambda to: g_late.at[0, outer, to], lambda at: rq_late.at[at, 0, outer]
+    )
+    last_start(1 - half, lambda to: to != inmost)
+    second(far[0], 1, far[:1], g_late.at[0])
+    sq_late[0, inmost] = q_sum(
+        2, lambda to: g_late.at[0, inmost, to], lambda at: rq_late.at[at, 0, inmost]
+    )
+    last_start(1 - half, lambda to: to == inmost)
     last = (0, 0, 1 - half, sq_late.at[0])
-    last_start(*last)
 
     across(0, s_x.at[1 - zh]).wait_recv()
     put(s_x[zh].astype(F32) + r_across[0].astype(F32), fg_ref)
@@ -443,8 +454,8 @@
             pltpu.VMEM((2, 16, BS), BF16),
             pltpu.SemaphoreType.DMA((2, NBL)),
             pltpu.SemaphoreType.DMA((2, NBL)),
-            pltpu.SemaphoreType.DMA((2, 8)),
-            pltpu.SemaphoreType.DMA((2, 8)),
+            pltpu.SemaphoreType.DMA((3, 8)),
+            pltpu.SemaphoreType.DMA((3, 8)),
             pltpu.SemaphoreType.DMA((1, 4)),
             pltpu.SemaphoreType.DMA((1, 8)),
             pltpu.SemaphoreType.DMA((4,)),

time: 71.1 us -> 70.2 us (0.987)
  the two profiles are of different devices: /device:TPU:224 before, /device:TPU:230 now
where the time goes in v7:
time: 70.2 us; the launch traced here: 70.1 us
  Pallas kernels  69.5 us (99%)
    pallas_call x1, Pallas kernels, per_device(): pl.pallas_call(kernel, out_shape=(jax.ShapeDtypeStruct((NBL, 2, BS), F32)...  68.6 us

profile of v7, /device:TPU:230, one launch (start us, length us, event | category | flops | bytes accessed | tf_op | source)
XLA Modules:
  0.0 70.1 jit_solution(10979833667722920423)
XLA Ops:
  0.6 68.6 %shard_map.76 = (f32[8,2,128]{2,1,0:T(2,128)S(1)}, f32[8,2,128]{2,1,0:T(2,128)S(1)}, bf16[256,1024]{1,0:T(8,128)(2,1)S(1)}) custom-call(bf16[256,1024]{1,0:T(8,128)(2,1)} %x_hbm.1, bf16[8,128,128]{2,1,0:T(8,128)(2,1)} %w_hbm.1, bf16[8,128,128]{2,1,0:T(8,128)(2,1)} %l_hbm.1, s32[1,64]{1,0:T(1,128)} %bitcast.1, bf16[256,1024]{1,0:T(8,128)(2,1)} %og_hbm.1), custom_call_target="tpu_custom_call" | custom-call | tf_op jit(solution)/shard_map/pallas_call | solution.py:420
  69.3 0.8 %shard_map.77 = (f32[8,2,128]{2,1,0:T(2,128)}, f32[8,2,128]{2,1,0:T(2,128)}, bf16[256,1024]{1,0:T(8,128)(2,1)}) custom-call(f32[8,2,128]{2,1,0:T(2,128)S(1)} %get-tuple-element.6.fg_in, f32[8,2,128]{2,1,0:T(2,128)S(1)} %get-tuple-element.7.lg_in, bf16[256,1024]{1,0:T(8,128)(2,1)S(1)} %get-tuple-element.8.ig_in), custom_call_target="tpu_custom_call" | custom-call | tf_op jit(solution)/shard_map/pallas_call | solution.py:475

commit v8 on v7

--- a/solution.py
+++ b/solution.py
@@ -180,12 +180,12 @@
     pair = one_hot(iota(1)[:64] // 2 == iota(0)[:64])
     target = dot_nn(perm, pair)[:1] * 2.0 + (iota(1)[:1] % 2).astype(F32)
     placing = one_hot(iota(0).astype(F32) == target)
-    for k in range(2, 6):
-        activation(2 * k - 4)
-        activation(2 * k - 3)
+    for k in range(2, 4):
         entered(k)
-    entered(6)
-    entered(7)
+    for a in range(8):
+        activation(a)
+    for k in range(4, 8):
+        entered(k)
     recv_mg[:, slab(b), :] = swapped(tmp, b)
 
     @pl.when(at_edge)
@@ -239,7 +239,7 @@
         )
 
     def q_sum(n, src, land):
-        for k in range(1, 8):
+        for k in (4, 5, 3, 2, 6, 7, 1):
             to = (q + k) % 8
             c = copy(rs_send, rs_recv, n, to, q, src(to), land(q), q_peer(k))
             c.start()

time: 70.2 us -> 70.1 us (level)
  no operation moved by 1% of the time
where the time goes in v8:
time: 70.1 us; the launch traced here: 69.9 us
  Pallas kernels  69.3 us (99%)
    pallas_call x1, Pallas kernels, per_device(): pl.pallas_call(kernel, out_shape=(jax.ShapeDtypeStruct((NBL, 2, BS), F32)...  68.5 us

profile of v8, /device:TPU:230, one launch (start us, length us, event | category | flops | bytes accessed | tf_op | source)
XLA Modules:
  0.0 69.9 jit_solution(8170189754008668038)
XLA Ops:
  0.6 68.5 %shard_map.76 = (f32[8,2,128]{2,1,0:T(2,128)S(1)}, f32[8,2,128]{2,1,0:T(2,128)S(1)}, bf16[256,1024]{1,0:T(8,128)(2,1)S(1)}) custom-call(bf16[256,1024]{1,0:T(8,128)(2,1)} %x_hbm.1, bf16[8,128,128]{2,1,0:T(8,128)(2,1)} %w_hbm.1, bf16[8,128,128]{2,1,0:T(8,128)(2,1)} %l_hbm.1, s32[1,64]{1,0:T(1,128)} %bitcast.1, bf16[256,1024]{1,0:T(8,128)(2,1)} %og_hbm.1), custom_call_target="tpu_custom_call" | custom-call | tf_op jit(solution)/shard_map/pallas_call | solution.py:420
  69.1 0.8 %shard_map.77 = (f32[8,2,128]{2,1,0:T(2,128)}, f32[8,2,128]{2,1,0:T(2,128)}, bf16[256,1024]{1,0:T(8,128)(2,1)}) custom-call(f32[8,2,128]{2,1,0:T(2,128)S(1)} %get-tuple-element.6.fg_in, f32[8,2,128]{2,1,0:T(2,128)S(1)} %get-tuple-element.7.lg_in, bf16[256,1024]{1,0:T(8,128)(2,1)S(1)} %get-tuple-element.8.ig_in), custom_call_target="tpu_custom_call" | custom-call | tf_op jit(solution)/shard_map/pallas_call | solution.py:475

commit v9 on v7

--- a/solution.py
+++ b/solution.py
@@ -239,7 +239,7 @@
         )
 
     def q_sum(n, src, land):
-        for k in range(1, 8):
+        for k in (4, 5, 3, 2, 6, 7, 1):
             to = (q + k) % 8
             c = copy(rs_send, rs_recv, n, to, q, src(to), land(q), q_peer(k))
             c.start()

time: 70.2 us -> 70.1 us (level)
  no operation moved by 1% of the time
where the time goes in v9:
time: 70.1 us; the launch traced here: 70 us
  Pallas kernels  69.4 us (99%)
    pallas_call x1, Pallas kernels, per_device(): pl.pallas_call(kernel, out_shape=(jax.ShapeDtypeStruct((NBL, 2, BS), F32)...  68.5 us

profile of v9, /device:TPU:230, one launch (start us, length us, event | category | flops | bytes accessed | tf_op | source)
XLA Modules:
  0.0 70.0 jit_solution(15211112151161152430)
XLA Ops:
  0.6 68.5 %shard_map.76 = (f32[8,2,128]{2,1,0:T(2,128)S(1)}, f32[8,2,128]{2,1,0:T(2,128)S(1)}, bf16[256,1024]{1,0:T(8,128)(2,1)S(1)}) custom-call(bf16[256,1024]{1,0:T(8,128)(2,1)} %x_hbm.1, bf16[8,128,128]{2,1,0:T(8,128)(2,1)} %w_hbm.1, bf16[8,128,128]{2,1,0:T(8,128)(2,1)} %l_hbm.1, s32[1,64]{1,0:T(1,128)} %bitcast.1, bf16[256,1024]{1,0:T(8,128)(2,1)} %og_hbm.1), custom_call_target="tpu_custom_call" | custom-call | tf_op jit(solution)/shard_map/pallas_call | solution.py:420
  69.2 0.8 %shard_map.77 = (f32[8,2,128]{2,1,0:T(2,128)}, f32[8,2,128]{2,1,0:T(2,128)}, bf16[256,1024]{1,0:T(8,128)(2,1)}) custom-call(f32[8,2,128]{2,1,0:T(2,128)S(1)} %get-tuple-element.6.fg_in, f32[8,2,128]{2,1,0:T(2,128)S(1)} %get-tuple-element.7.lg_in, bf16[256,1024]{1,0:T(8,128)(2,1)S(1)} %get-tuple-element.8.ig_in), custom_call_target="tpu_custom_call" | custom-call | tf_op jit(solution)/shard_map/pallas_call | solution.py:475
